TPU v7x, 32 devices: a whole 2x2x4 slice. The times are simulated.
32 devices in a mesh: groups: 2 (over y), row: 4 (over z), col: 4 (over x, core).
Axes of the slice: x: 2, y: 2, z: 4, core: 2. Of those that a mesh axis runs over, the one named last changes fastest.
Arguments:
- positions: float32 [4096, 3, 128], P(('groups', 'row', 'col')), parts along dimension 0, may hold values from -6 to 6
- normals: float32 [4096, 3, 128], P(('groups', 'row', 'col')), parts along dimension 0, may hold values from -6 to 6
- curvature: float32 [4096, 128], P(('groups', 'row', 'col')), parts along dimension 0, may hold values from 0.5 to 3
- pair_targets: int32 [32, 512], P(('groups', 'row', 'col')), parts along dimension 0, may hold values from 0 to 511, as said below
- pair_sources: int32 [32, 512], P(('groups', 'row', 'col')), parts along dimension 0, may hold values from 0 to 511
- pair_count: int32 [32], P(('groups', 'row', 'col')), parts along dimension 0, may hold values from 64 to 512, as said below
- node_counts: int32 [512, 8], P('groups'), parts along dimension 0, may hold values from 1 to 128, 642 in all within a row
- drop_clusters: int32 [512, 8], P('groups'), parts along dimension 0, may hold values from 0 to 2047, as said below
- drop_owner: int32 [512], P('groups'), parts along dimension 0, may hold values from 0 to 15, as said below
Outputs:
- drop_velocity: float32 [4096, 3, 128], P(('groups', 'row', 'col')), parts along dimension 0
There are 2 independent parts, one for each index of `groups`. A program takes and returns all parts, laid end to end along the dimension named above; each array names one. Nothing has to cross between parts.
Inputs may be any that keep to these rules, and one draw needn't show every extreme that they name: `drop_clusters`: every cluster of 0 to 2047 appears exactly once. Of the 128 clusters of one device, at most 16 belong to drops of any one owner, and this many is reached. `drop_owner`: every device owns exactly 16 drops. `pair_count`: the largest count is reached on some device; list entries past a device's count are not pairs. In each device's list, at most 256 entries have the same value of pair_targets // 128, and every device's list reaches this many for some value. `node_counts`: each drop's counts sum to 642.
All inputs are finite; a program needn't handle non-finite values.
Results may differ from a plain program's by a relative error of at most 0.0003.
Values sent between devices are 32-bit elements; how exact they have to be, the bound alone decides.
A program may use at most 64 MiB of HBM per device.

v0:
```python
import functools
import math

import jax
import jax.numpy as jnp
from jax import lax
from jax.experimental import pallas as pl
from jax.experimental.pallas import tpu as pltpu
from jax.sharding import PartitionSpec as P

regular_sq = 0.0025
stokes_scale = 1.0 / (8.0 * math.pi)
MESH = pl.DeviceIdType.MESH
VMEM = pl.BlockSpec(memory_space=pltpu.VMEM)
SMEM = pl.BlockSpec(memory_space=pltpu.SMEM)


unroll = 32


def gather_kernel(nrow, ncol, pos_ref, nrm_ref, curv_ref, cnt_ref, t_ref, s_ref, tsend, trecv, ssend, srecv):
    row, col = lax.axis_index("row"), lax.axis_index("col")
    barrier = pltpu.get_barrier_semaphore()
    for d in range(1, nrow):
        pl.semaphore_signal(barrier, inc=1, device_id={"row": lax.rem(row + d, nrow)}, device_id_type=MESH)
    for d in range(1, ncol):
        pl.semaphore_signal(barrier, inc=1, device_id={"col": lax.rem(col + d, ncol)}, device_id_type=MESH)
    live = lax.broadcasted_iota(jnp.int32, curv_ref.shape, 1) < cnt_ref[...]
    scale = jnp.where(live, curv_ref[...], 0.0)
    for k in range(3):
        coord = pos_ref[k]
        t_ref[col, k] = coord
        s_ref[row, k] = coord
        s_ref[row, 3 + k] = scale * nrm_ref[k]
    pl.semaphore_wait(barrier, nrow + ncol - 2)
    copies = []
    for d in range(1, ncol):
        copies.append(pltpu.make_async_remote_copy(
            src_ref=t_ref.at[col], dst_ref=t_ref.at[col],
            send_sem=tsend.at[d - 1], recv_sem=trecv.at[d - 1],
            device_id={"col": lax.rem(col + d, ncol)}, device_id_type=MESH))

    def relay(way, step):
        block = jnp.clip(row - way * step, 0, nrow - 1)
        to = jnp.clip(row + way, 0, nrow - 1)
        at = step if way > 0 else nrow - 1 + step
        return pltpu.make_async_remote_copy(
            src_ref=s_ref.at[block], dst_ref=s_ref.at[block],
            send_sem=ssend.at[at], recv_sem=srecv.at[at],
            device_id={"row": to}, device_id_type=MESH)

    def sends(way, step):
        return (row < nrow - 1) & (row >= step) if way > 0 else (row > 0) & (row + step < nrow)

    def receives(way, step):
        return row >= step + 1 if way > 0 else row + step + 1 < nrow

    for step in range(nrow - 1):
        for way in (1, -1):
            if step > 0:
                @pl.when(receives(way, step - 1))
                def _():
                    relay(way, step - 1).wait_recv()

            @pl.when(sends(way, step))
            def _():
                relay(way, step).start()
        if step == 0:
            for copy in copies:
                copy.start()
    for way in (1, -1):
        @pl.when(receives(way, nrow - 2))
        def _():
            relay(way, nrow - 2).wait_recv()
        for step in range(nrow - 1):
            @pl.when(sends(way, step))
            def _():
                relay(way, step).wait_send()
    for copy in copies:
        copy.wait()


def split3(x):
    high = x.astype(jnp.bfloat16).astype(jnp.float32)
    rest = x - high
    middle = rest.astype(jnp.bfloat16).astype(jnp.float32)
    return high, middle, rest - middle


def split2(x):
    high = x.astype(jnp.bfloat16)
    return high, (x - high.astype(jnp.float32)).astype(jnp.bfloat16)


def pair_kernel(tgt_ref, src_ref, count_ref, t_ref, s_ref, v_ref, tc_ref, sc_ref):
    ncol, _, local, _ = t_ref.shape
    nrow = s_ref.shape[0]
    slots = tgt_ref.shape[1]
    f32 = jnp.float32
    v_ref[...] = jnp.zeros_like(v_ref)

    def targets(c, carry):
        rows = pl.ds(pl.multiple_of(c * local, local), local)
        square = jnp.full((local, 128), regular_sq, f32)
        for k in range(3):
            coord = t_ref[c, k]
            centre = jnp.mean(coord, axis=1, keepdims=True)
            coord = coord - centre
            square = square + coord * coord
            tc_ref[rows, k, :] = coord
            tc_ref[rows, 5 + k, :] = jnp.broadcast_to(centre, coord.shape)
        tc_ref[rows, 3, :] = square
        tc_ref[rows, 4, :] = jnp.ones((local, 128), f32)
        return carry

    lax.fori_loop(0, ncol, targets, 0)

    def sources(r, carry):
        rows = pl.ds(pl.multiple_of(r * local, local), local)
        for k in range(6):
            sc_ref[rows, k, :] = s_ref[r, k]
        return carry

    lax.fori_loop(0, nrow, sources, 0)
    count = count_ref[0]
    ones = jnp.ones((1, 128), f32)
    none = jnp.zeros((3, 128), f32)

    def many(block, carry):
        made = []
        for u in range(unroll):
            e = block * unroll + u
            active = e < count
            e = jnp.minimum(e, slots - 1)
            t, s = tgt_ref[0, e], src_ref[0, e]
            near = tc_ref[t]
            far = sc_ref[s]
            shifted = far[0:3] - near[5:8]
            force = jnp.where(active, far[3:6], 0.0)
            square = jnp.sum(shifted * shifted, axis=0, keepdims=True)
            along = jnp.sum(shifted * force, axis=0, keepdims=True)
            a_hi, a_mid, a_lo = split3(jnp.concatenate([near[0:5], none], axis=0))
            b_hi, b_mid, b_lo = split3(jnp.concatenate([-2.0 * shifted, ones, square, none], axis=0))
            c_hi, c_mid, c_lo = split3(jnp.concatenate([force, 0.0 * ones, -along, none], axis=0))
            right = jnp.concatenate([a_hi, a_mid, a_lo, a_hi, a_mid, a_hi], axis=0).astype(jnp.bfloat16)
            left = jnp.concatenate([
                jnp.concatenate([b_hi, b_hi, b_hi, b_mid, b_mid, b_lo], axis=0),
                jnp.concatenate([c_hi, c_hi, c_hi, c_mid, c_mid, c_lo], axis=0)], axis=1).astype(jnp.bfloat16)
            both = lax.dot_general(left, right, (((0,), (0,)), ((), ())), preferred_element_type=f32)
            gathered = jnp.concatenate([force, shifted, ones, ones], axis=0)
            g_hi = gathered.astype(jnp.bfloat16).astype(f32)
            g = jnp.concatenate([g_hi, gathered - g_hi], axis=0).astype(jnp.bfloat16)
            made.append((t, near, both, g))
        results = []
        for t, near, both, g in made:
            inv = lax.rsqrt(both[0:128])
            weight = inv * inv * inv
            iso_hi, iso_lo = split2(inv + regular_sq * weight)
            pro_hi, pro_lo = split2(both[128:256] * weight)
            m = jnp.concatenate([
                jnp.concatenate([iso_hi, pro_hi], axis=1), jnp.concatenate([iso_lo, pro_lo], axis=1)], axis=0)
            out = jnp.dot(jnp.concatenate([g, g], axis=1), m, preferred_element_type=f32)
            out = out[0:8] + out[8:16]
            results.append((t, stokes_scale * (out[0:3, 0:128] + near[0:3] * out[6:7, 128:256] - out[3:6, 128:256])))
        for t, speed in results:
            c, i = t // local, lax.rem(t, local)
            for k in range(3):
                v_ref[c, k, pl.ds(i, 1), :] += speed[k:k + 1]
        return carry

    lax.fori_loop(0, (count + unroll - 1) // unroll, many, 0)


def home_kernel(nrow, ncol, cap, pack_ref, from_ref, rank_ref, cnt_ref, v_ref, out_ref, got, part, home, outg, arr, vsend, vrecv, asend, arecv):
    row, col = lax.axis_index("row"), lax.axis_index("col")
    local = out_ref.shape[1]
    devs = nrow * ncol
    me = row * ncol + col
    barrier = pltpu.get_barrier_semaphore()

    def peer(d):
        p = lax.rem(me + d, devs)
        return {"row": p // ncol, "col": lax.rem(p, ncol)}

    for d in range(1, devs):
        pl.semaphore_signal(barrier, inc=1, device_id=peer(d), device_id_type=MESH)
    pl.semaphore_wait(barrier, devs - 1)
    half = ncol // 2
    core = lax.rem(col, 2)
    mine_x = col // 2
    within, across = [], []
    for d in [*range(1, half), 0]:
        x = lax.rem(mine_x + d, half)
        within.append(pltpu.make_async_remote_copy(
            src_ref=v_ref.at[2 * x + 1 - core], dst_ref=got.at[d], send_sem=vsend.at[d], recv_sem=vrecv.at[d],
            device_id={"col": col + 1 - 2 * core}, device_id_type=MESH))
    for copy in within:
        copy.start()
    for d in range(1, half):
        to = 2 * lax.rem(mine_x + d, half) + core
        within[d - 1].wait_recv()
        part[d - 1] = v_ref[to] + got[d]
        copy = pltpu.make_async_remote_copy(
            src_ref=part.at[d - 1], dst_ref=got.at[half + d - 1],
            send_sem=vsend.at[half + d - 1], recv_sem=vrecv.at[half + d - 1],
            device_id={"col": to}, device_id_type=MESH)
        copy.start()
        across.append(copy)
    within[half - 1].wait_recv()
    for copy in across:
        copy.wait_recv()
    for k in range(3):
        mine = v_ref[col, k] + got[0, k]
        for d in range(1, half):
            mine = mine + got[half + d - 1, k]
        home[:, k, :] = mine
    for copy in within + across:
        copy.wait_send()

    def pack(p, carry):
        for j in range(cap):
            one = home[pack_ref[p * cap + j]]
            for k in range(3):
                outg[p, k, j:j + 1, :] = one[k:k + 1]
        return carry

    lax.fori_loop(0, devs, pack, 0)
    copies = []
    for d in range(1, devs):
        copies.append(pltpu.make_async_remote_copy(
            src_ref=outg.at[lax.rem(me + d, devs)], dst_ref=arr.at[me],
            send_sem=asend.at[d - 1], recv_sem=arecv.at[d - 1],
            device_id=peer(d), device_id_type=MESH))
    for copy in copies:
        copy.start()
    arr[me] = outg[me]
    for copy in copies:
        copy.wait()
    slots = lax.broadcasted_iota(jnp.int32, (1, 128), 1)

    def unpack(i, carry):
        for u in range(8):
            n = i * 8 + u
            at, place = from_ref[n], rank_ref[n]
            live = slots < cnt_ref[n]
            for k in range(3):
                out_ref[k, pl.ds(n, 1), :] = jnp.where(live, arr[at, k, pl.ds(place, 1), :], 0.0)
        return carry

    lax.fori_loop(0, local // 8, unpack, 0)


def per_device(positions, normals, curvature, pair_targets, pair_sources, pair_count, node_counts, drop_clusters, drop_owner):
    local, _, nodes = positions.shape
    nrow, ncol = lax.axis_size("row"), lax.axis_size("col")
    devs = nrow * ncol
    me = lax.axis_index("row") * ncol + lax.axis_index("col")
    cap = max(2, 2 * local // devs)
    per_drop = drop_clusters.shape[1]
    drops = drop_owner.shape[0]
    here = local // per_drop
    ints = jnp.int32

    flat_clusters = drop_clusters.T.reshape(-1)
    flat_counts = node_counts.T.reshape(-1)
    flat_owner = jnp.broadcast_to(drop_owner[None, :], (per_drop, drops)).reshape(-1)
    order = jnp.arange(local, dtype=ints)
    hit = (me * local + order)[:, None] == flat_clusters[None, :]
    home_counts = jnp.sum(jnp.where(hit, flat_counts[None, :], 0), axis=1, dtype=ints)
    home_owner = jnp.sum(jnp.where(hit, flat_owner[None, :], 0), axis=1, dtype=ints)
    rank = jnp.sum((home_owner[None, :] == home_owner[:, None]) & (order[None, :] < order[:, None]), axis=1, dtype=ints)
    slot_of = home_owner * cap + rank
    all_slots = jnp.arange(devs * cap, dtype=ints)
    pack = jnp.sum(jnp.where(slot_of[None, :] == all_slots[:, None], order[None, :], 0), axis=1, dtype=ints)

    drop_ids = jnp.arange(drops, dtype=ints)
    mine = drop_owner == me
    place = jnp.sum(mine[None, :] & (drop_ids[None, :] < drop_ids[:, None]), axis=1, dtype=ints)
    chosen = mine[None, :] & (place[None, :] == jnp.arange(here, dtype=ints)[:, None])
    owned_clusters = jnp.sum(jnp.where(chosen[:, :, None], drop_clusters[None], 0), axis=1, dtype=ints).reshape(-1)
    owned_counts = jnp.sum(jnp.where(chosen[:, :, None], node_counts[None], 0), axis=1, dtype=ints).reshape(-1)
    anchor = owned_clusters // local
    before = (anchor[None, :] == anchor[:, None]) & (owned_clusters[None, :] < owned_clusters[:, None])
    place_in = jnp.sum(before, axis=1, dtype=ints)

    dma = pltpu.SemaphoreType.DMA
    f32 = jnp.float32
    targets, sources = pl.pallas_call(
        functools.partial(gather_kernel, nrow, ncol),
        out_shape=(jax.ShapeDtypeStruct((ncol, 3, local, nodes), f32), jax.ShapeDtypeStruct((nrow, 6, local, nodes), f32)),
        in_specs=[VMEM] * 4, out_specs=(VMEM, VMEM),
        scratch_shapes=[dma((ncol - 1,)), dma((ncol - 1,)), dma((2 * nrow - 2,)), dma((2 * nrow - 2,))],
        compiler_params=pltpu.CompilerParams(collective_id=0, has_side_effects=True, vmem_limit_bytes=56 << 20),
        name="gather_blocks",
    )(jnp.transpose(positions, (1, 0, 2)), jnp.transpose(normals, (1, 0, 2)), curvature, home_counts[:, None])
    speeds = pl.pallas_call(
        pair_kernel,
        out_shape=jax.ShapeDtypeStruct((ncol, 3, local, nodes), f32),
        in_specs=[SMEM] * 3 + [VMEM] * 2, out_specs=VMEM,
        scratch_shapes=[pltpu.VMEM((ncol * local, 8, nodes), f32), pltpu.VMEM((nrow * local, 8, nodes), f32)],
        compiler_params=pltpu.CompilerParams(vmem_limit_bytes=56 << 20),
        name="pairs",
    )(pair_targets, pair_sources, pair_count, targets, sources)
    owned = pl.pallas_call(
        functools.partial(home_kernel, nrow, ncol, cap),
        out_shape=jax.ShapeDtypeStruct((3, local, nodes), f32),
        in_specs=[SMEM] * 4 + [VMEM], out_specs=VMEM,
        scratch_shapes=[
            pltpu.VMEM((ncol - 1, 3, local, nodes), f32), pltpu.VMEM((max(ncol // 2 - 1, 1), 3, local, nodes), f32),
            pltpu.VMEM((local, 8, nodes), f32),
            pltpu.VMEM((devs, 3, cap, nodes), f32), pltpu.VMEM((devs, 3, cap, nodes), f32),
            dma((ncol - 1,)), dma((ncol - 1,)), dma((devs - 1,)), dma((devs - 1,)),
        ],
        compiler_params=pltpu.CompilerParams(collective_id=1, has_side_effects=True, vmem_limit_bytes=56 << 20),
        name="to_owners",
    )(pack, anchor, place_in, owned_counts, speeds)
    return jnp.transpose(owned, (1, 0, 2))


def solution(mesh):
    every = ("groups", "row", "col")
    in_specs = (
        P(every, None, None), P(every, None, None), P(every, None), P(every, None), P(every, None), P(every),
        P("groups", None), P("groups", None), P("groups"),
    )
    return jax.shard_map(per_device, mesh=mesh, in_specs=in_specs, out_specs=P(every, None, None), check_vma=False)
```

profile of v0, /device:TPU:15, one launch (start us, length us, event | category | flops | bytes accessed | tf_op | source)
XLA Modules:
  0.0 95.6 jit_solution(6246586480567449983)
XLA Ops:
  0.7 0.7 broadcast_compare_fusion
  1.3 0.1 convert_reduce_fusion
  1.5 0.7 copy.17
  2.2 0.7 copy.19
  2.9 0.7 broadcast_bitcast_fusion
  3.6 0.3 fusion.1
  3.9 0.2 convert_reduce_fusion.2
  4.1 0.7 select_reduce_fusion.2.pack_ref
  4.8 1.3 %select_reduce_fusion = (s32[16,8]{1,0:T(8,128)S(1)}, s32[16,8]{1,0:T(8,128)S(1)}) fusion(s32[256,8]{0,1:T(8,128)} %param.15, pred[16,256]{1,0:T(8,128)(4,1)S(1)} %fusion.4, s32[256,8]{0,1:T(8,128)} %param.16), kind=kLoop, calls=%fused_computation.7 | loop fusion | flops 130816 | bytes 21504 | tf_op jit(solution)/shard_map/reduce_sum | solution.py:281
  6.1 0.6 reshape.113.cnt_ref
  6.7 0.1 reshape.112
  6.8 0.0 copy-start
  6.8 0.8 convert_reduce_fusion.1.rank_ref
  7.6 0.7 copy.16.cnt_ref
  8.4 30.4 %gather_blocks.1 = (f32[4,3,128,128]{3,2,1,0:T(8,128)}, f32[4,6,128,128]{3,2,1,0:T(8,128)}) custom-call(f32[3,128,128]{2,1,0:T(8,128)} %bitcast.14, f32[3,128,128]{2,1,0:T(8,128)} %bitcast.15, f32[128,128]{1,0:T(8,128)} %curv_ref.1, s32[128,1]{1,0:T(8,128)} %copy.16.cnt_ref), custom_call_target="tpu_custom_call" | custom-call | tf_op jit(solution)/shard_map/gather_blocks/pallas_call | solution.py:288
  38.7 11.8 %pairs.1.v_ref = f32[4,3,128,128]{3,2,1,0:T(8,128)} custom-call(s32[1,512]{1,0:T(1,128)} %tgt_ref.1, s32[1,512]{1,0:T(1,128)} %src_ref.1, s32[1]{0:T(128)S(6)} %copy.21.count_ref, f32[4,3,128,128]{3,2,1,0:T(8,128)} %get-tuple-element.7.t_ref, f32[4,6,128,128]{3,2,1,0:T(8,128)} %get-tuple-element.8.s_ref), custom_call_target="tpu_custom_call" | custom-call | tf_op jit(solution)/shard_map/pairs/pallas_call | solution.py:296
  50.5 0.0 copy-done
  50.5 43.5 %to_owners.1 = f32[3,128,128]{2,1,0:T(8,128)} custom-call(s32[256]{0:T(256)} %select_reduce_fusion.2.pack_ref, s32[128]{0:T(128)} %copy-done, s32[128]{0:T(128)} %convert_reduce_fusion.1.rank_ref, s32[128]{0:T(128)} %reshape.113.cnt_ref, f32[4,3,128,128]{3,2,1,0:T(8,128)} %pairs.1.v_ref), custom_call_target="tpu_custom_call" | custom-call | tf_op jit(solution)/shard_map/to_owners/pallas_call | solution.py:304
  94.0 1.6 %copy.22 = f32[128,3,128]{2,0,1:T(8,128)} copy(f32[128,3,128]{2,0,1:T(8,128)} %bitcast.13) | data formatting | bytes 393216
  (5 shorter events, 0.0 us)
Async XLA Ops:
  6.8 43.7 %copy-start = (s32[128]{0:T(128)}, s32[128]{0:T(128)S(1)}, u32[]{:S(2)}) copy-start(s32[128]{0:T(128)S(1)} %and_select_fusion.from_ref) | copy-start | bytes 1540
where the time goes:
time: 97.1 us; the launch traced here: 95.6 us
  Pallas kernels  85.6 us (88%)
  local copies, waits for them, and re-layouts  5.14 us (5%)
  other arithmetic  4.13 us (4%)
    pallas_call x1, Pallas kernels, per_device(): pl.pallas_call(functools.partial(home_kernel, nrow, ncol, cap), out_shape...  43.5 us
    pallas_call x1, Pallas kernels, per_device(): pl.pallas_call(functools.partial(gather_kernel, nrow, ncol), out_shape=(j...  30.4 us
    pallas_call x1, Pallas kernels, per_device(): pl.pallas_call(pair_kernel, out_shape=jax.ShapeDtypeStruct((ncol, 3, loca...  11.8 us
    unnamed x7, local copies, waits for them, and re-layouts  3.71 us

commit v1 on v0

v1 whole, which is shorter than its diff:
```python
import functools
import math

import jax
import jax.numpy as jnp
from jax import lax
from jax.experimental import pallas as pl
from jax.experimental.pallas import tpu as pltpu
from jax.sharding import PartitionSpec as P

regular_sq = 0.0025
inv_reg = 1.0 / math.sqrt(regular_sq)
stokes_scale = inv_reg / (8.0 * math.pi)
MESH = pl.DeviceIdType.MESH
VMEM = pl.BlockSpec(memory_space=pltpu.VMEM)
SMEM = pl.BlockSpec(memory_space=pltpu.SMEM)


unroll = 16
f32, bf16, ints = jnp.float32, jnp.bfloat16, jnp.int32


def keep(x):
    return pltpu.with_memory_space_constraint(x, pltpu.VMEM)


def split3(x):
    high = x.astype(bf16).astype(f32)
    rest = x - high
    middle = rest.astype(bf16).astype(f32)
    return high, middle, rest - middle


def as_row(column):
    return jnp.transpose(jnp.broadcast_to(column, (column.shape[0], 128)))[0:1]


def gather_kernel(
        nrow, ncol, cap, pos_ref, nrm_ref, curv_ref, nct_ref, dct_ref, own_ref, tgt_ref, src_ref, count_ref,
        near_ref, right_ref, far_ref, lt_ref, ls_ref, lc_ref, pack_ref, from_ref, rank_ref, cnt_ref,
        t_ref, s_ref, tsend, trecv, zsend, zrecv, fsend, frecv, osend, orecv, lsend, lrecv):
    row, col = lax.axis_index("row"), lax.axis_index("col")
    core = lax.rem(col, 2)
    other = col + 1 - 2 * core
    me = row * ncol + col
    local = pos_ref.shape[1]
    drops = own_ref.shape[1]
    per_drop = dct_ref.shape[0]
    barrier = pltpu.get_barrier_semaphore()
    for d in range(1, nrow):
        pl.semaphore_signal(barrier, inc=1, device_id={"row": lax.rem(row + d, nrow)}, device_id_type=MESH)
    for d in range(1, ncol):
        pl.semaphore_signal(barrier, inc=1, device_id={"col": lax.rem(col + d, ncol)}, device_id_type=MESH)
    for k in range(3):
        s_ref[core, row, k] = pos_ref[k]
    lt_ref[core] = tgt_ref[...]
    ls_ref[core] = src_ref[...]
    lc_ref[core] = jnp.full((1, 128), count_ref[0], ints)

    def remote(src, dst, send, recv, where):
        return pltpu.make_async_remote_copy(
            src_ref=src, dst_ref=dst, send_sem=send, recv_sem=recv, device_id=where, device_id_type=MESH)

    sibling = {"col": other}
    small = [remote(ref.at[core], ref.at[core], lsend.at[i], lrecv.at[i], sibling)
             for i, ref in enumerate((lt_ref, ls_ref, lc_ref))]
    rows = [remote(pos_ref, t_ref.at[col], tsend.at[d - 1], trecv.at[d - 1], {"col": lax.rem(col + d, ncol)})
            for d in range(1, ncol)]

    def along(d, k):
        piece = s_ref.at[core, row, k]
        return remote(piece, piece, zsend.at[d - 1, k], zrecv.at[d - 1, k], {"row": lax.rem(row + d, nrow)})

    def arrived(d, k):
        return s_ref.at[core, lax.rem(row + nrow - d, nrow), k]

    def onward(d, k):
        piece = arrived(d, k)
        return remote(piece, piece, fsend.at[d - 1, k], frecv.at[d - 1, k], sibling)

    def own(k):
        piece = s_ref.at[core, row, k]
        return remote(piece, piece, osend.at[k], orecv.at[k], sibling)

    pl.semaphore_wait(barrier, nrow + ncol - 2)
    for k in range(3):
        for d in range(1, nrow):
            along(d, k).start()
    for copy in small + rows:
        copy.start()

    index = lax.broadcasted_iota(ints, (local, 1), 0)
    ids = me * local + index

    def match(chunk, carry):
        counts, owners = carry
        lanes = pl.ds(pl.multiple_of(chunk * 128, 128), 128)
        clusters, nodes_in, owner = dct_ref[:, lanes], nct_ref[:, lanes], own_ref[0:1, lanes]
        for k in range(per_drop):
            hit = ids == clusters[k:k + 1]
            counts = counts + jnp.where(hit, nodes_in[k:k + 1], 0)
            owners = owners + jnp.where(hit, owner, 0)
        return counts, owners

    none = jnp.zeros((local, 128), ints)
    counts, owners = lax.fori_loop(0, drops // 128, match, (none, none))
    home_counts = jnp.sum(counts, axis=1, keepdims=True, dtype=ints)
    home_owner = jnp.sum(owners, axis=1, keepdims=True, dtype=ints)
    scale = jnp.where(lax.broadcasted_iota(ints, (local, 128), 1) < home_counts, curv_ref[...], 0.0)
    for k in range(3):
        s_ref[core, row, 3 + k] = scale * nrm_ref[k]
        for d in range(1, nrow):
            along(d, 3 + k).start()
    for k in range(6):
        own(k).start()

    owner_row = as_row(home_owner.astype(f32)).astype(ints)
    lane = lax.broadcasted_iota(ints, (local, local), 1)
    rank = jnp.sum(((owner_row == home_owner) & (lane < index)).astype(ints), axis=1, keepdims=True, dtype=ints)
    slot = home_owner * cap + rank
    slots = lax.broadcasted_iota(ints, pack_ref.shape, 1)
    pack_ref[...] = jnp.sum(jnp.where(slot == slots, index, 0), axis=0, keepdims=True, dtype=ints)

    here = lax.broadcasted_iota(ints, (local, 1), 0)
    drop_of = lax.div(here, per_drop)
    width = 256 if drops % 256 == 0 else 128
    before = (lax.broadcasted_iota(ints, (width, width), 0) < lax.broadcasted_iota(ints, (width, width), 1)).astype(bf16)

    def owned(chunk, carry):
        clusters, counted, base = carry
        lanes = pl.ds(pl.multiple_of(chunk * width, width), width)
        mine = own_ref[0:1, lanes] == me
        marks = jnp.broadcast_to(mine.astype(f32), (16, width)).astype(bf16)
        place = jnp.dot(marks, before, preferred_element_type=f32)[0:1].astype(ints) + base
        chosen = mine & (place == drop_of)
        clusters = clusters + jnp.where(chosen, jnp.concatenate([dct_ref[:, lanes]] * (local // per_drop), axis=0), 0)
        counted = counted + jnp.where(chosen, jnp.concatenate([nct_ref[:, lanes]] * (local // per_drop), axis=0), 0)
        return clusters, counted, base + jnp.sum(mine.astype(ints), axis=1, keepdims=True, dtype=ints)

    wide = jnp.zeros((local, width), ints)
    clusters, counted, _ = lax.fori_loop(0, drops // width, owned, (wide, wide, jnp.zeros((1, 1), ints)))
    clusters = jnp.sum(clusters, axis=1, keepdims=True, dtype=ints)
    cnt_ref[...] = as_row(jnp.sum(counted, axis=1, keepdims=True, dtype=ints).astype(f32)).astype(ints)
    clusters_row = as_row(clusters.astype(f32)).astype(ints)
    anchor, anchor_row = lax.div(clusters, local), lax.div(clusters_row, local)
    from_ref[...] = anchor_row
    rank_ref[...] = jnp.sum(((anchor == anchor_row) & (clusters < clusters_row)).astype(ints), axis=0, keepdims=True, dtype=ints)

    def fill(i, carry):
        base = pl.multiple_of(i * 64, 64)
        far_ref[pl.ds(base, 64), :] = jnp.zeros((64, 128), f32)
        return carry

    lax.fori_loop(0, far_ref.shape[0] // 64, fill, 0)

    def spread(l, r, k):
        at = (l * nrow + r) * local * 8 + (k if k < 3 else k + 1)
        far_ref[pl.ds(at, local, stride=8), :] = s_ref[l, r, k]

    for k in range(6):
        spread(core, row, k)

    sub = lax.broadcasted_iota(ints, (8, 128), 0)
    low = sub < 4

    def targets(d):
        c = lax.rem(col + ncol - d, ncol)
        square = jnp.ones((local, 128), f32)
        start = c * local * 8
        for k in range(3):
            coord = pos_ref[k] if d == 0 else t_ref[c, k]
            centre = jnp.mean(coord, axis=1, keepdims=True)
            coord = (coord - centre) * inv_reg
            square = square + coord * coord
            near_ref[pl.ds(start + k, local, stride=8), :] = coord
            near_ref[pl.ds(start + 4 + k, local, stride=8), :] = jnp.broadcast_to(centre, coord.shape)
        near_ref[pl.ds(start + 3, local, stride=8), :] = square
        near_ref[pl.ds(start + 7, local, stride=8), :] = jnp.zeros((local, 128), f32)

        def coefficients(i, carry):
            for u in range(8):
                t = c * local + i * 8 + u
                tile = near_ref[pl.ds(pl.multiple_of(t * 8, 8), 8), :]
                high, middle, rest = split3(tile)
                sums = jnp.where(sub == 0, high[3:4], jnp.where(sub == 1, middle[3:4], jnp.where(sub == 2, rest[3:4], 0.0)))
                high = jnp.where(sub < 3, high, jnp.where(sub == 3, 1.0, 0.0))
                middle = jnp.where(sub < 3, middle, 0.0)
                rest = jnp.where(sub < 3, rest, 0.0)
                high_up, middle_up = pltpu.roll(high, 4, 0), pltpu.roll(middle, 4, 0)
                right_ref[t] = jnp.concatenate([
                    high + middle_up, rest + high_up, middle + high_up, sums], axis=0).astype(bf16)
            return carry

        lax.fori_loop(0, local // 8, coefficients, 0)

    targets(0)
    for d in range(1, ncol):
        rows[d - 1].wait_recv()
        targets(d)
    for k in range(6):
        own(k).wait_recv()
        spread(1 - core, row, k)
    for k in range(6):
        for d in range(1, nrow):
            along(d, k).wait_recv()
            onward(d, k).start()
            spread(core, lax.rem(row + nrow - d, nrow), k)
    for k in range(6):
        for d in range(1, nrow):
            onward(d, k).wait_recv()
            spread(1 - core, lax.rem(row + nrow - d, nrow), k)
    for copy in small:
        copy.wait()
    for copy in rows:
        copy.wait_send()
    for k in range(6):
        own(k).wait_send()
        for d in range(1, nrow):
            along(d, k).wait_send()
            onward(d, k).wait_send()


def pair_kernel(lt_ref, ls_ref, lc_ref, near_ref, right_ref, far_ref, v_ref, acc_ref, both_a, both_b, g_a, g_b):
    ncol, _, local, _ = v_ref.shape
    half_far = far_ref.shape[0] // 16
    core = lax.rem(lax.axis_index("col"), 2)
    sub = lax.broadcasted_iota(ints, (8, 128), 0)
    low = sub < 4
    last = (sub == 3) | (sub == 7)
    scale = jnp.where(low, -2.0, 1.0).astype(f32)
    fold = jnp.where(sub == 3, 1.0, jnp.where(sub == 7, -1.0, 0.0)).astype(f32)
    some = jnp.where(low, 1.0, 0.0).astype(f32)
    unit = jnp.where(low, inv_reg, 1.0).astype(f32)
    idle = jnp.where(low, inv_reg, 0.0).astype(f32)
    nothing = jnp.zeros((32, 128), bf16)
    acc_ref[...] = jnp.zeros_like(acc_ref)
    both_b[...] = jnp.ones_like(both_b)
    g_b[...] = jnp.zeros_like(g_b)
    n0 = lc_ref[0, 0, 0]
    total = n0 + lc_ref[1, 0, 0]
    half = (total + 1) // 2
    first = core * half
    n = jnp.where(core == 0, half, total - half)

    def entry(j):
        j = first + jnp.clip(j, 0, n - 1)
        second = j >= n0
        return second.astype(ints), jnp.where(second, j - n0, j)

    def tile(i):
        return pl.ds(pl.multiple_of(i * 8, 8), 8)

    def distances(block, both_ref, g_ref):
        for u in range(unroll):
            j = block * unroll + u
            l, e = entry(j)
            t, s = lt_ref[l, 0, e], ls_ref[l, 0, e] + l * half_far
            centre = jnp.where(low, pltpu.roll(near_ref[tile(t), :], 4, 0), 0.0)
            right = right_ref[t]
            shifted = (far_ref[tile(s), :] - centre) * jnp.where(j < n, unit, idle)
            prod = shifted * jnp.where(low, shifted, pltpu.roll(shifted, 4, 0))
            prod = prod + pltpu.roll(prod, 1, 0)
            prod = prod + pltpu.roll(prod, 2, 0)
            hi, mid, lo = split3(shifted * scale + prod * fold)
            hi_up, mid_up, lo_up = pltpu.roll(hi, 4, 0), pltpu.roll(mid, 4, 0), pltpu.roll(lo, 4, 0)
            left = jnp.concatenate([
                jnp.where(low, hi, hi_up), jnp.where(low, hi, mid_up), jnp.where(low, mid, lo_up), some,
                jnp.where(low, hi_up, hi), jnp.where(low, hi_up, mid), jnp.where(low, mid_up, lo),
                jnp.zeros((8, 128), f32)], axis=0).astype(bf16)
            weights = jnp.concatenate([
                jnp.concatenate([right, nothing], axis=1), jnp.concatenate([nothing, right], axis=1)], axis=0)
            both_ref[u] = lax.dot_general(left, weights, (((0,), (0,)), ((), ())), preferred_element_type=f32)
            g_ref[u] = jnp.concatenate([jnp.where(last, 1.0, hi), jnp.where(last, 0.0, mid)], axis=0).astype(bf16)

    def speeds(block, both_ref, g_ref):
        for u in range(unroll):
            l, e = entry(block * unroll + u)
            t = lt_ref[l, 0, e]
            both, g = both_ref[u], g_ref[u]
            inv = lax.rsqrt(both[:, 0:128])
            weight = inv * inv * inv
            iso = inv + weight
            pro = both[:, 128:256] * weight
            iso_hi, pro_hi = iso.astype(bf16), pro.astype(bf16)
            iso_lo = (iso - iso_hi.astype(f32)).astype(bf16)
            pro_lo = (pro - pro_hi.astype(f32)).astype(bf16)
            m = jnp.concatenate([
                jnp.concatenate([iso_hi, pro_hi], axis=1), jnp.concatenate([iso_lo, pro_lo], axis=1)], axis=0)
            out = jnp.dot(jnp.concatenate([g, g], axis=1), m, preferred_element_type=f32)
            out = out[0:8] + out[8:16]
            from_iso, from_pro = out[:, 0:128], out[:, 128:256]
            acc_ref[tile(t), :] += pltpu.roll(from_iso, 4, 0) + near_ref[tile(t), :] * from_pro[3:4] + 0.5 * from_pro

    def many(i, carry):
        distances(2 * i, both_a, g_a)
        speeds(2 * i - 1, both_b, g_b)
        distances(2 * i + 1, both_b, g_b)
        speeds(2 * i, both_a, g_a)
        return carry

    lax.fori_loop(0, (n + unroll - 1) // unroll // 2 + 1, many, 0)
    for c in range(ncol):
        for k in range(3):
            v_ref[c, k] = stokes_scale * acc_ref[pl.ds(c * local * 8 + k, local, stride=8), :]


def home_kernel(nrow, ncol, cap, pack_ref, from_ref, rank_ref, cnt_ref, v_ref, out_ref, got, part, home, outg, arr, vsend, vrecv, asend, arecv):
    row, col = lax.axis_index("row"), lax.axis_index("col")
    local = out_ref.shape[1]
    devs = nrow * ncol
    me = row * ncol + col
    barrier = pltpu.get_barrier_semaphore()

    def peer(d):
        p = lax.rem(me + d, devs)
        return {"row": p // ncol, "col": lax.rem(p, ncol)}

    for d in range(1, devs):
        pl.semaphore_signal(barrier, inc=1, device_id=peer(d), device_id_type=MESH)
    pl.semaphore_wait(barrier, devs - 1)
    half = ncol // 2
    core = lax.rem(col, 2)
    mine_x = col // 2
    within, across = [], []
    for d in [*range(1, half), 0]:
        x = lax.rem(mine_x + d, half)
        within.append(pltpu.make_async_remote_copy(
            src_ref=v_ref.at[2 * x + 1 - core], dst_ref=got.at[d], send_sem=vsend.at[d], recv_sem=vrecv.at[d],
            device_id={"col": col + 1 - 2 * core}, device_id_type=MESH))
    for copy in within:
        copy.start()
    for d in range(1, half):
        to = 2 * lax.rem(mine_x + d, half) + core
        within[d - 1].wait_recv()
        part[d - 1] = v_ref[to] + got[d]
        copy = pltpu.make_async_remote_copy(
            src_ref=part.at[d - 1], dst_ref=got.at[half + d - 1],
            send_sem=vsend.at[half + d - 1], recv_sem=vrecv.at[half + d - 1],
            device_id={"col": to}, device_id_type=MESH)
        copy.start()
        across.append(copy)
    within[half - 1].wait_recv()
    for copy in across:
        copy.wait_recv()
    for k in range(3):
        mine = v_ref[col, k] + got[0, k]
        for d in range(1, half):
            mine = mine + got[half + d - 1, k]
        home[:, k, :] = mine
    for copy in within + across:
        copy.wait_send()

    def pack(p, carry):
        for j in range(cap):
            one = home[pack_ref[0, p * cap + j]]
            for k in range(3):
                outg[p, k, j:j + 1, :] = one[k:k + 1]
        return carry

    lax.fori_loop(0, devs, pack, 0)
    copies = []
    for d in range(1, devs):
        copies.append(pltpu.make_async_remote_copy(
            src_ref=outg.at[lax.rem(me + d, devs)], dst_ref=arr.at[me],
            send_sem=asend.at[d - 1], recv_sem=arecv.at[d - 1],
            device_id=peer(d), device_id_type=MESH))
    for copy in copies:
        copy.start()
    arr[me] = outg[me]
    for copy in copies:
        copy.wait()
    slots = lax.broadcasted_iota(jnp.int32, (1, 128), 1)

    def unpack(i, carry):
        for u in range(8):
            n = i * 8 + u
            at, place = from_ref[0, n], rank_ref[0, n]
            live = slots < cnt_ref[0, n]
            for k in range(3):
                out_ref[k, pl.ds(n, 1), :] = jnp.where(live, arr[at, k, pl.ds(place, 1), :], 0.0)
        return carry

    lax.fori_loop(0, local // 8, unpack, 0)


def per_device(positions, normals, curvature, pair_targets, pair_sources, pair_count, node_counts, drop_clusters, drop_owner):
    local, _, nodes = positions.shape
    nrow, ncol = lax.axis_size("row"), lax.axis_size("col")
    devs = nrow * ncol
    cap = max(2, 2 * local // devs)
    slots = pair_targets.shape[1]
    dma = pltpu.SemaphoreType.DMA
    shape = jax.ShapeDtypeStruct
    near, right, far, lt, ls, lc, pack, anchor, place_in, owned_counts = pl.pallas_call(
        functools.partial(gather_kernel, nrow, ncol, cap),
        out_shape=(
            pltpu.VMEM((ncol * local * 8, nodes), f32), pltpu.VMEM((ncol * local, 32, nodes), bf16),
            pltpu.VMEM((2 * nrow * local * 8, nodes), f32),
            shape((2, 1, slots), ints), shape((2, 1, slots), ints), shape((2, 1, 128), ints),
            shape((1, devs * cap), ints), shape((1, local), ints), shape((1, local), ints), shape((1, local), ints)),
        in_specs=[VMEM] * 8 + [SMEM], out_specs=(VMEM,) * 10,
        scratch_shapes=[
            pltpu.VMEM((ncol, 3, local, nodes), f32), pltpu.VMEM((2, nrow, 6, local, nodes), f32),
            dma((ncol - 1,)), dma((ncol - 1,)), dma((nrow - 1, 6)), dma((nrow - 1, 6)), dma((nrow - 1, 6)), dma((nrow - 1, 6)),
            dma((6,)), dma((6,)), dma((3,)), dma((3,))],
        compiler_params=pltpu.CompilerParams(collective_id=0, has_side_effects=True, vmem_limit_bytes=24 << 20),
        name="gather_blocks",
    )(jnp.transpose(positions, (1, 0, 2)), jnp.transpose(normals, (1, 0, 2)), curvature, node_counts.T, drop_clusters.T,
      drop_owner[None, :], pair_targets, pair_sources, pair_count)
    speeds = pl.pallas_call(
        pair_kernel,
        out_shape=pltpu.VMEM((ncol, 3, local, nodes), f32),
        in_specs=[SMEM] * 3 + [VMEM] * 3, out_specs=VMEM,
        scratch_shapes=[pltpu.VMEM((ncol * local * 8, nodes), f32)]
        + [pltpu.VMEM((unroll, nodes, 2 * nodes), f32)] * 2 + [pltpu.VMEM((unroll, 16, nodes), bf16)] * 2,
        compiler_params=pltpu.CompilerParams(vmem_limit_bytes=24 << 20),
        name="pairs",
    )(lt, ls, lc, keep(near), keep(right), keep(far))
    owned = pl.pallas_call(
        functools.partial(home_kernel, nrow, ncol, cap),
        out_shape=jax.ShapeDtypeStruct((3, local, nodes), f32),
        in_specs=[SMEM] * 4 + [VMEM], out_specs=VMEM,
        scratch_shapes=[
            pltpu.VMEM((ncol - 1, 3, local, nodes), f32), pltpu.VMEM((max(ncol // 2 - 1, 1), 3, local, nodes), f32),
            pltpu.VMEM((local, 8, nodes), f32),
            pltpu.VMEM((devs, 3, cap, nodes), f32), pltpu.VMEM((devs, 3, cap, nodes), f32),
            dma((ncol - 1,)), dma((ncol - 1,)), dma((devs - 1,)), dma((devs - 1,)),
        ],
        compiler_params=pltpu.CompilerParams(collective_id=1, has_side_effects=True, vmem_limit_bytes=24 << 20),
        name="to_owners",
    )(pack, anchor, place_in, owned_counts, keep(speeds))
    return jnp.transpose(owned, (1, 0, 2))


def solution(mesh):
    every = ("groups", "row", "col")
    in_specs = (
        P(every, None, None), P(every, None, None), P(every, None), P(every, None), P(every, None), P(every),
        P("groups", None), P("groups", None), P("groups"),
    )
    return jax.shard_map(per_device, mesh=mesh, in_specs=in_specs, out_specs=P(every, None, None), check_vma=False)
```

time: 97.1 us -> 87.3 us (0.90)
  the two profiles are of different devices: /device:TPU:15 before, /device:TPU:0 now
where the time goes in v1:
time: 87.3 us; the launch traced here: 86.3 us
  Pallas kernels  78.8 us (90%)
  local copies, waits for them, and re-layouts  6.8 us (8%)
    pallas_call x1, Pallas kernels, per_device(): pl.pallas_call(functools.partial(gather_kernel, nrow, ncol, cap), out_sha...  41.2 us
    pallas_call x1, Pallas kernels, per_device(): pl.pallas_call(functools.partial(home_kernel, nrow, ncol, cap), out_shape...  28.4 us
    pallas_call x1, Pallas kernels, per_device(): pl.pallas_call(pair_kernel, out_shape=pltpu.VMEM((ncol, 3, local, nodes),...  9.22 us
    unnamed x17, local copies, waits for them, and re-layouts  6.8 us

profile of v1, /device:TPU:0, one launch (start us, length us, event | category | flops | bytes accessed | tf_op | source)
XLA Modules:
  0.0 86.3 jit_solution(6563794177931477197)
XLA Ops:
  0.7 0.0 copy-start
  0.7 0.9 %copy-done = f32[128,3,128]{2,0,1:T(8,128)S(1)} copy-done((f32[128,3,128]{2,0,1:T(8,128)S(1)}, f32[128,3,128]{2,0,1:T(8,128)}, u32[]{:S(2)}) %copy-start) | copy-done | bytes 196632
  1.6 0.0 copy-start.1
  1.6 0.9 %copy-done.1 = f32[128,3,128]{2,0,1:T(8,128)S(1)} copy-done((f32[128,3,128]{2,0,1:T(8,128)S(1)}, f32[128,3,128]{2,0,1:T(8,128)}, u32[]{:S(2)}) %copy-start.1) | copy-done | bytes 196632
  2.5 0.0 copy-start.2
  2.5 0.8 copy-done.2
  3.3 0.0 copy-start.3
  3.3 0.7 copy-done.3
  4.0 0.0 copy-start.4
  4.0 0.7 copy-done.4
  4.7 0.0 copy-start.5
  4.7 0.7 copy-done.5
  5.4 0.0 copy-start.6
  5.4 0.7 copy-done.6
  6.1 0.0 copy-start.7
  6.1 0.7 copy-done.7
  6.8 41.2 %gather_blocks.1 = (f32[4096,128]{1,0:T(8,128)S(1)}, bf16[512,32,128]{2,1,0:T(8,128)(2,1)S(1)}, f32[8192,128]{1,0:T(8,128)S(1)}, s32[2,1,512]{2,1,0:T(1,128)S(1)...) custom-call(f32[3,128,128]{2,1,0:T(8,128)S(1)} %bitcast.7, ...), custom_call_target="tpu_custom_call" | custom-call | tf_op jit(solution)/shard_map/gather_blocks/pallas_call | solution.py:394
  48.0 9.2 %pairs.1.v_ref = f32[4,3,128,128]{3,2,1,0:T(8,128)S(1)} custom-call(s32[2,1,512]{2,1,0:T(1,128)S(1)} %get-tuple-element.19.lt_ref, s32[2,1,512]{2,1,0:T(1,128)S(1)} %get-tuple-element.20.ls_ref, s32[2,1,128]{2,1,0:T(1,128)S(1)} %get-tuple-element.21.lc_ref, f32[4096,128]{1,0:T(8,128)S(1)} %get-tuple-element.22.near_ref, ...), custom_call_target="tpu_custom_call" | custom-call | tf_op jit(solution)/shard_map/pairs/pallas_call | solution.py:410
  57.3 28.4 %to_owners.1 = f32[3,128,128]{2,1,0:T(8,128)S(1)} custom-call(s32[1,256]{1,0:T(1,128)S(1)} %get-tuple-element.15.pack_ref, s32[1,128]{1,0:T(1,128)S(1)} %get-tuple-element.16.from_ref, s32[1,128]{1,0:T(1,128)S(1)} %get-tuple-element.17.rank_ref, s32[1,128]{1,0:T(1,128)S(1)} %get-tuple-element.18.cnt_ref, f32[4,3,128,128]{3,2,1,0:T(8,128)S(1)} %pairs.1.v_ref), custom_call_target="tpu_custom_call" | custom-call | tf_op jit(solution)/shard_map/to_owners/pallas_call | solution.py:419
  85.7 0.7 copy.12
Async XLA Ops:
  0.7 0.9 %copy-start = (f32[128,3,128]{2,0,1:T(8,128)S(1)}, f32[128,3,128]{2,0,1:T(8,128)}, u32[]{:S(2)}) copy-start(f32[128,3,128]{2,0,1:T(8,128)} %param.9) | copy-start | bytes 589828
  1.6 0.9 %copy-start.1 = (f32[128,3,128]{2,0,1:T(8,128)S(1)}, f32[128,3,128]{2,0,1:T(8,128)}, u32[]{:S(2)}) copy-start(f32[128,3,128]{2,0,1:T(8,128)} %param.10) | copy-start | bytes 589828
  2.5 0.8 copy-start.2
  3.3 0.7 copy-start.3
  4.0 0.7 copy-start.4
  4.7 0.7 copy-start.5
  5.4 0.7 copy-start.6
  6.1 0.7 copy-start.7

commit v2 on v1

--- a/solution.py
+++ b/solution.py
@@ -16,12 +16,17 @@
 SMEM = pl.BlockSpec(memory_space=pltpu.SMEM)
 
 
+HBM = pl.BlockSpec(memory_space=pltpu.HBM)
 unroll = 16
 f32, bf16, ints = jnp.float32, jnp.bfloat16, jnp.int32
 
 
 def keep(x):
     return pltpu.with_memory_space_constraint(x, pltpu.VMEM)
+
+
+def far_off(x):
+    return pltpu.with_memory_space_constraint(x, pltpu.HBM)
 
 
 def split3(x):
@@ -36,25 +41,27 @@
 
 
 def gather_kernel(
-        nrow, ncol, cap, pos_ref, nrm_ref, curv_ref, nct_ref, dct_ref, own_ref, tgt_ref, src_ref, count_ref,
+        nrow, ncol, cap, pos_in, nrm_in, curv_in, nct_in, dct_in, own_in, tgt_in, src_in, count_ref,
         near_ref, right_ref, far_ref, lt_ref, ls_ref, lc_ref, pack_ref, from_ref, rank_ref, cnt_ref,
-        t_ref, s_ref, tsend, trecv, zsend, zrecv, fsend, frecv, osend, orecv, lsend, lrecv):
+        nrm_ref, curv_ref, nct_ref, dct_ref, own_ref, here_sem, t_ref, s_ref, tsend, trecv, zsend, zrecv, fsend, frecv, osend, orecv, lsend, lrecv):
     row, col = lax.axis_index("row"), lax.axis_index("col")
     core = lax.rem(col, 2)
     other = col + 1 - 2 * core
     me = row * ncol + col
-    local = pos_ref.shape[1]
+    local = pos_in.shape[1]
     drops = own_ref.shape[1]
     per_drop = dct_ref.shape[0]
+    pos_ref = s_ref.at[core, row, 0:3]
+    loads = [pltpu.make_async_copy(src, dst, here_sem.at[i]) for i, (src, dst) in enumerate((
+        (pos_in, pos_ref), (dct_in, dct_ref), (nct_in, nct_ref), (own_in, own_ref), (curv_in, curv_ref), (nrm_in, nrm_ref),
+        (tgt_in, lt_ref.at[core]), (src_in, ls_ref.at[core])))]
+    for load in loads:
+        load.start()
     barrier = pltpu.get_barrier_semaphore()
     for d in range(1, nrow):
         pl.semaphore_signal(barrier, inc=1, device_id={"row": lax.rem(row + d, nrow)}, device_id_type=MESH)
     for d in range(1, ncol):
         pl.semaphore_signal(barrier, inc=1, device_id={"col": lax.rem(col + d, ncol)}, device_id_type=MESH)
-    for k in range(3):
-        s_ref[core, row, k] = pos_ref[k]
-    lt_ref[core] = tgt_ref[...]
-    ls_ref[core] = src_ref[...]
     lc_ref[core] = jnp.full((1, 128), count_ref[0], ints)
 
     def remote(src, dst, send, recv, where):
@@ -67,26 +74,44 @@
     rows = [remote(pos_ref, t_ref.at[col], tsend.at[d - 1], trecv.at[d - 1], {"col": lax.rem(col + d, ncol)})
             for d in range(1, ncol)]
 
-    def along(d, k):
-        piece = s_ref.at[core, row, k]
-        return remote(piece, piece, zsend.at[d - 1, k], zrecv.at[d - 1, k], {"row": lax.rem(row + d, nrow)})
-
-    def arrived(d, k):
-        return s_ref.at[core, lax.rem(row + nrow - d, nrow), k]
-
-    def onward(d, k):
-        piece = arrived(d, k)
-        return remote(piece, piece, fsend.at[d - 1, k], frecv.at[d - 1, k], sibling)
+    def block_of(way, step):
+        return jnp.clip(row - way * step, 0, nrow - 1)
+
+    def relay(way, step, k):
+        piece = s_ref.at[core, block_of(way, step), k]
+        at = step if way > 0 else nrow - 1 + step
+        return remote(piece, piece, zsend.at[at, k], zrecv.at[at, k], {"row": jnp.clip(row + way, 0, nrow - 1)})
+
+    def sends(way, step):
+        return (row < nrow - 1) & (row >= step) if way > 0 else (row > 0) & (row + step < nrow)
+
+    def receives(way, step):
+        return row >= step + 1 if way > 0 else row + step + 1 < nrow
+
+    def onward(way, step, k):
+        piece = s_ref.at[core, block_of(way, step + 1), k]
+        at = step if way > 0 else nrow - 1 + step
+        return remote(piece, piece, fsend.at[at, k], frecv.at[at, k], sibling)
+
+    def start(way, step, k):
+        @pl.when(sends(way, step))
+        def _():
+            relay(way, step, k).start()
 
     def own(k):
         piece = s_ref.at[core, row, k]
         return remote(piece, piece, osend.at[k], orecv.at[k], sibling)
 
+    loads[0].wait()
     pl.semaphore_wait(barrier, nrow + ncol - 2)
     for k in range(3):
-        for d in range(1, nrow):
-            along(d, k).start()
-    for copy in small + rows:
+        for way in (1, -1):
+            start(way, 0, k)
+    for copy in rows:
+        copy.start()
+    for load in loads[1:]:
+        load.wait()
+    for copy in small:
         copy.start()
 
     index = lax.broadcasted_iota(ints, (local, 1), 0)
@@ -109,8 +134,8 @@
     scale = jnp.where(lax.broadcasted_iota(ints, (local, 128), 1) < home_counts, curv_ref[...], 0.0)
     for k in range(3):
         s_ref[core, row, 3 + k] = scale * nrm_ref[k]
-        for d in range(1, nrow):
-            along(d, 3 + k).start()
+        for way in (1, -1):
+            start(way, 0, 3 + k)
     for k in range(6):
         own(k).start()
 
@@ -168,7 +193,7 @@
         square = jnp.ones((local, 128), f32)
         start = c * local * 8
         for k in range(3):
-            coord = pos_ref[k] if d == 0 else t_ref[c, k]
+            coord = s_ref[core, row, k] if d == 0 else t_ref[c, k]
             centre = jnp.mean(coord, axis=1, keepdims=True)
             coord = (coord - centre) * inv_reg
             square = square + coord * coord
@@ -200,24 +225,38 @@
     for k in range(6):
         own(k).wait_recv()
         spread(1 - core, row, k)
-    for k in range(6):
-        for d in range(1, nrow):
-            along(d, k).wait_recv()
-            onward(d, k).start()
-            spread(core, lax.rem(row + nrow - d, nrow), k)
-    for k in range(6):
-        for d in range(1, nrow):
-            onward(d, k).wait_recv()
-            spread(1 - core, lax.rem(row + nrow - d, nrow), k)
+    for step in range(nrow - 1):
+        for k in range(6):
+            for way in (1, -1):
+                @pl.when(receives(way, step))
+                def _():
+                    relay(way, step, k).wait_recv()
+                    if step < nrow - 2:
+                        start(way, step + 1, k)
+                    onward(way, step, k).start()
+                    spread(core, block_of(way, step + 1), k)
+    for step in range(nrow - 1):
+        for k in range(6):
+            for way in (1, -1):
+                @pl.when(receives(way, step))
+                def _():
+                    onward(way, step, k).wait_recv()
+                    spread(1 - core, block_of(way, step + 1), k)
     for copy in small:
         copy.wait()
     for copy in rows:
         copy.wait_send()
     for k in range(6):
         own(k).wait_send()
-        for d in range(1, nrow):
-            along(d, k).wait_send()
-            onward(d, k).wait_send()
+        for step in range(nrow - 1):
+            for way in (1, -1):
+                @pl.when(sends(way, step))
+                def _():
+                    relay(way, step, k).wait_send()
+
+                @pl.when(receives(way, step))
+                def _():
+                    onward(way, step, k).wait_send()
 
 
 def pair_kernel(lt_ref, ls_ref, lc_ref, near_ref, right_ref, far_ref, v_ref, acc_ref, both_a, both_b, g_a, g_b):
@@ -398,15 +437,17 @@
             pltpu.VMEM((2 * nrow * local * 8, nodes), f32),
             shape((2, 1, slots), ints), shape((2, 1, slots), ints), shape((2, 1, 128), ints),
             shape((1, devs * cap), ints), shape((1, local), ints), shape((1, local), ints), shape((1, local), ints)),
-        in_specs=[VMEM] * 8 + [SMEM], out_specs=(VMEM,) * 10,
+        in_specs=[HBM] * 8 + [SMEM], out_specs=(VMEM,) * 10,
         scratch_shapes=[
+            pltpu.VMEM((3, local, nodes), f32), pltpu.VMEM((local, nodes), f32), *[pltpu.VMEM(drop_clusters.shape[::-1], ints)] * 2,
+            pltpu.VMEM((1, drop_owner.shape[0]), ints), dma((8,)),
             pltpu.VMEM((ncol, 3, local, nodes), f32), pltpu.VMEM((2, nrow, 6, local, nodes), f32),
-            dma((ncol - 1,)), dma((ncol - 1,)), dma((nrow - 1, 6)), dma((nrow - 1, 6)), dma((nrow - 1, 6)), dma((nrow - 1, 6)),
+            dma((ncol - 1,)), dma((ncol - 1,)), *[dma((2 * nrow - 2, 6))] * 4,
             dma((6,)), dma((6,)), dma((3,)), dma((3,))],
         compiler_params=pltpu.CompilerParams(collective_id=0, has_side_effects=True, vmem_limit_bytes=24 << 20),
         name="gather_blocks",
-    )(jnp.transpose(positions, (1, 0, 2)), jnp.transpose(normals, (1, 0, 2)), curvature, node_counts.T, drop_clusters.T,
-      drop_owner[None, :], pair_targets, pair_sources, pair_count)
+    )(*map(far_off, (jnp.transpose(positions, (1, 0, 2)), jnp.transpose(normals, (1, 0, 2)), curvature, node_counts.T,
+                     drop_clusters.T, drop_owner[None, :], pair_targets, pair_sources)), pair_count)
     speeds = pl.pallas_call(
         pair_kernel,
         out_shape=pltpu.VMEM((ncol, 3, local, nodes), f32),

time: 87.3 us -> 72.8 us (0.83)
  Pallas kernels: 78.8 us -> 71.3 us
  local copies, waits for them, and re-layouts: 6.8 us -> 0.68 us
    pallas_call x1, Pallas kernels: 28.4 us -> 18.8 us  [per_device(): pl.pallas_call(functools.partial(home_kernel, nrow, ncol, cap), out_shape...]
    pallas_call x1, Pallas kernels: 9.22 us -> 17.3 us  [per_device(): pl.pallas_call(pair_kernel, out_shape=pltpu.VMEM((ncol, 3, local, nodes),...]
    pallas_call x1, Pallas kernels: 41.2 us -> 35.1 us  [per_device(): pl.pallas_call(functools.partial(gather_kernel, nrow, ncol, cap), out_sha...]
    unnamed x17 -> x1, local copies, waits for them, and re-layouts: 6.8 us -> 0.68 us
where the time goes in v2:
time: 72.8 us; the launch traced here: 72.6 us
  Pallas kernels  71.3 us (98%)
    pallas_call x1, Pallas kernels, per_device(): pl.pallas_call(functools.partial(gather_kernel, nrow, ncol, cap), out_sha...  35.1 us
    pallas_call x1, Pallas kernels, per_device(): pl.pallas_call(functools.partial(home_kernel, nrow, ncol, cap), out_shape...  18.8 us
    pallas_call x1, Pallas kernels, per_device(): pl.pallas_call(pair_kernel, out_shape=pltpu.VMEM((ncol, 3, local, nodes),...  17.3 us

profile of v2, /device:TPU:0, one launch (start us, length us, event | category | flops | bytes accessed | tf_op | source)
XLA Modules:
  0.0 72.6 jit_solution(13900951957517137065)
XLA Ops:
  0.7 35.1 %gather_blocks.1 = (f32[4096,128]{1,0:T(8,128)S(1)}, bf16[512,32,128]{2,1,0:T(8,128)(2,1)S(1)}, f32[8192,128]{1,0:T(8,128)S(1)}, s32[2,1,512]{2,1,0:T(1,128)S(1)...) custom-call(f32[3,128,128]{2,1,0:T(8,128)} %bitcast.7, ...), custom_call_target="tpu_custom_call" | custom-call | tf_op jit(solution)/shard_map/gather_blocks/pallas_call | solution.py:433
  35.8 17.3 %pairs.1.v_ref = f32[4,3,128,128]{3,2,1,0:T(8,128)S(1)} custom-call(s32[2,1,512]{2,1,0:T(1,128)S(1)} %get-tuple-element.19.lt_ref, s32[2,1,512]{2,1,0:T(1,128)S(1)} %get-tuple-element.20.ls_ref, s32[2,1,128]{2,1,0:T(1,128)S(1)} %get-tuple-element.21.lc_ref, f32[4096,128]{1,0:T(8,128)S(1)} %get-tuple-element.22.near_ref, ...), custom_call_target="tpu_custom_call" | custom-call | tf_op jit(solution)/shard_map/pairs/pallas_call | solution.py:451
  53.1 18.8 %to_owners.1 = f32[3,128,128]{2,1,0:T(8,128)S(1)} custom-call(s32[1,256]{1,0:T(1,128)S(1)} %get-tuple-element.15.pack_ref, s32[1,128]{1,0:T(1,128)S(1)} %get-tuple-element.16.from_ref, s32[1,128]{1,0:T(1,128)S(1)} %get-tuple-element.17.rank_ref, s32[1,128]{1,0:T(1,128)S(1)} %get-tuple-element.18.cnt_ref, f32[4,3,128,128]{3,2,1,0:T(8,128)S(1)} %pairs.1.v_ref), custom_call_target="tpu_custom_call" | custom-call | tf_op jit(solution)/shard_map/to_owners/pallas_call | solution.py:460
  71.9 0.7 copy.12

commit v3 on v2

--- a/solution.py
+++ b/solution.py
@@ -42,7 +42,7 @@
 
 def gather_kernel(
         nrow, ncol, cap, pos_in, nrm_in, curv_in, nct_in, dct_in, own_in, tgt_in, src_in, count_ref,
-        near_ref, right_ref, far_ref, lt_ref, ls_ref, lc_ref, pack_ref, from_ref, rank_ref, cnt_ref,
+        near_ref, right_ref, far_ref, lt_ref, ls_ref, lc_ref, slot_ref, place_ref, cnt_ref,
         nrm_ref, curv_ref, nct_ref, dct_ref, own_ref, here_sem, t_ref, s_ref, tsend, trecv, zsend, zrecv, fsend, frecv, osend, orecv, lsend, lrecv):
     row, col = lax.axis_index("row"), lax.axis_index("col")
     core = lax.rem(col, 2)
@@ -142,9 +142,7 @@
     owner_row = as_row(home_owner.astype(f32)).astype(ints)
     lane = lax.broadcasted_iota(ints, (local, local), 1)
     rank = jnp.sum(((owner_row == home_owner) & (lane < index)).astype(ints), axis=1, keepdims=True, dtype=ints)
-    slot = home_owner * cap + rank
-    slots = lax.broadcasted_iota(ints, pack_ref.shape, 1)
-    pack_ref[...] = jnp.sum(jnp.where(slot == slots, index, 0), axis=0, keepdims=True, dtype=ints)
+    slot_ref[...] = as_row((home_owner * cap + rank).astype(f32)).astype(ints)
 
     here = lax.broadcasted_iota(ints, (local, 1), 0)
     drop_of = lax.div(here, per_drop)
@@ -165,11 +163,11 @@
     wide = jnp.zeros((local, width), ints)
     clusters, counted, _ = lax.fori_loop(0, drops // width, owned, (wide, wide, jnp.zeros((1, 1), ints)))
     clusters = jnp.sum(clusters, axis=1, keepdims=True, dtype=ints)
-    cnt_ref[...] = as_row(jnp.sum(counted, axis=1, keepdims=True, dtype=ints).astype(f32)).astype(ints)
+    cnt_ref[...] = jnp.sum(counted, axis=1, keepdims=True, dtype=ints)
     clusters_row = as_row(clusters.astype(f32)).astype(ints)
     anchor, anchor_row = lax.div(clusters, local), lax.div(clusters_row, local)
-    from_ref[...] = anchor_row
-    rank_ref[...] = jnp.sum(((anchor == anchor_row) & (clusters < clusters_row)).astype(ints), axis=0, keepdims=True, dtype=ints)
+    same = (anchor == anchor_row) & (clusters_row < clusters)
+    place_ref[...] = anchor * cap + jnp.sum(same.astype(ints), axis=1, keepdims=True, dtype=ints)
 
     def fill(i, carry):
         base = pl.multiple_of(i * 64, 64)
@@ -343,7 +341,8 @@
             v_ref[c, k] = stokes_scale * acc_ref[pl.ds(c * local * 8 + k, local, stride=8), :]
 
 
-def home_kernel(nrow, ncol, cap, pack_ref, from_ref, rank_ref, cnt_ref, v_ref, out_ref, got, part, home, outg, arr, vsend, vrecv, asend, arecv):
+def home_kernel(
+        nrow, ncol, cap, slot_ref, place_ref, cnt_ref, v_ref, out_ref, got, part, outg, arr, vsend, vrecv, asend, arecv):
     row, col = lax.axis_index("row"), lax.axis_index("col")
     local = out_ref.shape[1]
     devs = nrow * ncol
@@ -356,70 +355,66 @@
 
     for d in range(1, devs):
         pl.semaphore_signal(barrier, inc=1, device_id=peer(d), device_id_type=MESH)
-    pl.semaphore_wait(barrier, devs - 1)
     half = ncol // 2
     core = lax.rem(col, 2)
     mine_x = col // 2
-    within, across = [], []
-    for d in [*range(1, half), 0]:
+
+    def remote(src, dst, send, recv, where):
+        return pltpu.make_async_remote_copy(
+            src_ref=src, dst_ref=dst, send_sem=send, recv_sem=recv, device_id=where, device_id_type=MESH)
+
+    def within(d, k):
         x = lax.rem(mine_x + d, half)
-        within.append(pltpu.make_async_remote_copy(
-            src_ref=v_ref.at[2 * x + 1 - core], dst_ref=got.at[d], send_sem=vsend.at[d], recv_sem=vrecv.at[d],
-            device_id={"col": col + 1 - 2 * core}, device_id_type=MESH))
-    for copy in within:
-        copy.start()
-    for d in range(1, half):
-        to = 2 * lax.rem(mine_x + d, half) + core
-        within[d - 1].wait_recv()
-        part[d - 1] = v_ref[to] + got[d]
-        copy = pltpu.make_async_remote_copy(
-            src_ref=part.at[d - 1], dst_ref=got.at[half + d - 1],
-            send_sem=vsend.at[half + d - 1], recv_sem=vrecv.at[half + d - 1],
-            device_id={"col": to}, device_id_type=MESH)
-        copy.start()
-        across.append(copy)
-    within[half - 1].wait_recv()
-    for copy in across:
-        copy.wait_recv()
-    for k in range(3):
+        return remote(v_ref.at[2 * x + 1 - core, k], got.at[d, k], vsend.at[d, k], vrecv.at[d, k], {"col": col + 1 - 2 * core})
+
+    def facing(d):
+        return 2 * lax.rem(mine_x + d, half) + core
+
+    def across(d, k):
+        at = half + d - 1
+        return remote(part.at[d - 1, k], got.at[at, k], vsend.at[at, k], vrecv.at[at, k], {"col": facing(d)})
+
+    def deal(d, k):
+        return remote(outg.at[k, lax.rem(me + d, devs)], arr.at[k, me], asend.at[d - 1, k], arecv.at[d - 1, k], peer(d))
+
+    def move(pick, values):
+        parts = jnp.concatenate(split3(values), axis=1).astype(bf16)
+        moved = jnp.dot(pick, parts, preferred_element_type=f32)
+        return moved[:, 0:128] + moved[:, 128:256] + moved[:, 256:384]
+
+    pick = (lax.broadcasted_iota(ints, (devs * cap, local), 0) == slot_ref[...]).astype(f32).astype(bf16)
+    pl.semaphore_wait(barrier, devs - 1)
+    for k in range(3):
+        for d in [*range(1, half), 0]:
+            within(d, k).start()
+    for k in range(3):
+        for d in range(1, half):
+            within(d, k).wait_recv()
+            part[d - 1, k] = v_ref[facing(d), k] + got[d, k]
+            across(d, k).start()
+    for k in range(3):
+        within(0, k).wait_recv()
         mine = v_ref[col, k] + got[0, k]
         for d in range(1, half):
+            across(d, k).wait_recv()
             mine = mine + got[half + d - 1, k]
-        home[:, k, :] = mine
-    for copy in within + across:
-        copy.wait_send()
-
-    def pack(p, carry):
-        for j in range(cap):
-            one = home[pack_ref[0, p * cap + j]]
-            for k in range(3):
-                outg[p, k, j:j + 1, :] = one[k:k + 1]
-        return carry
-
-    lax.fori_loop(0, devs, pack, 0)
-    copies = []
-    for d in range(1, devs):
-        copies.append(pltpu.make_async_remote_copy(
-            src_ref=outg.at[lax.rem(me + d, devs)], dst_ref=arr.at[me],
-            send_sem=asend.at[d - 1], recv_sem=arecv.at[d - 1],
-            device_id=peer(d), device_id_type=MESH))
-    for copy in copies:
-        copy.start()
-    arr[me] = outg[me]
-    for copy in copies:
-        copy.wait()
-    slots = lax.broadcasted_iota(jnp.int32, (1, 128), 1)
-
-    def unpack(i, carry):
-        for u in range(8):
-            n = i * 8 + u
-            at, place = from_ref[0, n], rank_ref[0, n]
-            live = slots < cnt_ref[0, n]
-            for k in range(3):
-                out_ref[k, pl.ds(n, 1), :] = jnp.where(live, arr[at, k, pl.ds(place, 1), :], 0.0)
-        return carry
-
-    lax.fori_loop(0, local // 8, unpack, 0)
+        outg[k] = move(pick, mine).reshape(devs, cap, 128)
+        for d in range(1, devs):
+            deal(d, k).start()
+        arr[k, me] = outg[k, me]
+    fetch = (lax.broadcasted_iota(ints, (local, devs * cap), 1) == place_ref[...]).astype(f32).astype(bf16)
+    live = lax.broadcasted_iota(ints, (local, 128), 1) < cnt_ref[...]
+    for k in range(3):
+        for d in range(1, devs):
+            deal(d, k).wait_recv()
+        out_ref[k] = jnp.where(live, move(fetch, arr[k].reshape(devs * cap, 128)), 0.0)
+    for k in range(3):
+        for d in range(half):
+            within(d, k).wait_send()
+        for d in range(1, half):
+            across(d, k).wait_send()
+        for d in range(1, devs):
+            deal(d, k).wait_send()
 
 
 def per_device(positions, normals, curvature, pair_targets, pair_sources, pair_count, node_counts, drop_clusters, drop_owner):
@@ -430,14 +425,14 @@
     slots = pair_targets.shape[1]
     dma = pltpu.SemaphoreType.DMA
     shape = jax.ShapeDtypeStruct
-    near, right, far, lt, ls, lc, pack, anchor, place_in, owned_counts = pl.pallas_call(
+    near, right, far, lt, ls, lc, slot, place, owned_counts = pl.pallas_call(
         functools.partial(gather_kernel, nrow, ncol, cap),
         out_shape=(
             pltpu.VMEM((ncol * local * 8, nodes), f32), pltpu.VMEM((ncol * local, 32, nodes), bf16),
             pltpu.VMEM((2 * nrow * local * 8, nodes), f32),
             shape((2, 1, slots), ints), shape((2, 1, slots), ints), shape((2, 1, 128), ints),
-            shape((1, devs * cap), ints), shape((1, local), ints), shape((1, local), ints), shape((1, local), ints)),
-        in_specs=[HBM] * 8 + [SMEM], out_specs=(VMEM,) * 10,
+            pltpu.VMEM((1, local), ints), pltpu.VMEM((local, 1), ints), pltpu.VMEM((local, 1), ints)),
+        in_specs=[HBM] * 8 + [SMEM], out_specs=(VMEM,) * 9,
         scratch_shapes=[
             pltpu.VMEM((3, local, nodes), f32), pltpu.VMEM((local, nodes), f32), *[pltpu.VMEM(drop_clusters.shape[::-1], ints)] * 2,
             pltpu.VMEM((1, drop_owner.shape[0]), ints), dma((8,)),
@@ -460,16 +455,15 @@
     owned = pl.pallas_call(
         functools.partial(home_kernel, nrow, ncol, cap),
         out_shape=jax.ShapeDtypeStruct((3, local, nodes), f32),
-        in_specs=[SMEM] * 4 + [VMEM], out_specs=VMEM,
+        in_specs=[VMEM] * 4, out_specs=VMEM,
         scratch_shapes=[
             pltpu.VMEM((ncol - 1, 3, local, nodes), f32), pltpu.VMEM((max(ncol // 2 - 1, 1), 3, local, nodes), f32),
-            pltpu.VMEM((local, 8, nodes), f32),
-            pltpu.VMEM((devs, 3, cap, nodes), f32), pltpu.VMEM((devs, 3, cap, nodes), f32),
-            dma((ncol - 1,)), dma((ncol - 1,)), dma((devs - 1,)), dma((devs - 1,)),
+            pltpu.VMEM((3, devs, cap, nodes), f32), pltpu.VMEM((3, devs, cap, nodes), f32),
+            dma((ncol - 1, 3)), dma((ncol - 1, 3)), dma((devs - 1, 3)), dma((devs - 1, 3)),
         ],
         compiler_params=pltpu.CompilerParams(collective_id=1, has_side_effects=True, vmem_limit_bytes=24 << 20),
         name="to_owners",
-    )(pack, anchor, place_in, owned_counts, keep(speeds))
+    )(keep(slot), keep(place), keep(owned_counts), keep(speeds))
     return jnp.transpose(owned, (1, 0, 2))
 
 

time: 72.8 us -> 73.4 us (level); the launches traced: 72.6 us -> 74 us
  Pallas kernels: 71.3 us -> 72.6 us
    pallas_call x1, Pallas kernels: 18.8 us -> 25 us  [per_device(): pl.pallas_call(functools.partial(home_kernel, nrow, ncol, cap), out_shape...]
    pallas_call x1, Pallas kernels: 17.3 us -> 12.5 us  [per_device(): pl.pallas_call(pair_kernel, out_shape=pltpu.VMEM((ncol, 3, local, nodes),...]
where the time goes in v3:
time: 73.4 us; the launch traced here: 74 us
  Pallas kernels  72.6 us (99%)
    pallas_call x1, Pallas kernels, per_device(): pl.pallas_call(functools.partial(gather_kernel, nrow, ncol, cap), out_sha...  35.1 us
    pallas_call x1, Pallas kernels, per_device(): pl.pallas_call(functools.partial(home_kernel, nrow, ncol, cap), out_shape...  25 us
    pallas_call x1, Pallas kernels, per_device(): pl.pallas_call(pair_kernel, out_shape=pltpu.VMEM((ncol, 3, local, nodes),...  12.5 us

profile of v3, /device:TPU:0, one launch (start us, length us, event | category | flops | bytes accessed | tf_op | source)
XLA Modules:
  0.0 74.0 jit_solution(6370326721853538798)
XLA Ops:
  0.7 35.1 %gather_blocks.1 = (f32[4096,128]{1,0:T(8,128)S(1)}, bf16[512,32,128]{2,1,0:T(8,128)(2,1)S(1)}, f32[8192,128]{1,0:T(8,128)S(1)}, s32[2,1,512]{2,1,0:T(1,128)S(1)...) custom-call(f32[3,128,128]{2,1,0:T(8,128)} %bitcast.7, ...), custom_call_target="tpu_custom_call" | custom-call | tf_op jit(solution)/shard_map/gather_blocks/pallas_call | solution.py:428
  35.8 12.5 %pairs.1.v_ref = f32[4,3,128,128]{3,2,1,0:T(8,128)S(1)} custom-call(s32[2,1,512]{2,1,0:T(1,128)S(1)} %get-tuple-element.17.lt_ref, s32[2,1,512]{2,1,0:T(1,128)S(1)} %get-tuple-element.18.ls_ref, s32[2,1,128]{2,1,0:T(1,128)S(1)} %get-tuple-element.19.lc_ref, f32[4096,128]{1,0:T(8,128)S(1)} %get-tuple-element.20.near_ref, ...), custom_call_target="tpu_custom_call" | custom-call | tf_op jit(solution)/shard_map/pairs/pallas_call | solution.py:446
  48.3 25.0 %to_owners.1 = f32[3,128,128]{2,1,0:T(8,128)S(1)} custom-call(s32[1,128]{1,0:T(1,128)S(1)} %get-tuple-element.14.slot_ref, s32[128,1]{1,0:T(8,128)S(1)} %get-tuple-element.15.place_ref, s32[128,1]{1,0:T(8,128)S(1)} %get-tuple-element.16.cnt_ref, f32[4,3,128,128]{3,2,1,0:T(8,128)S(1)} %pairs.1.v_ref), custom_call_target="tpu_custom_call" | custom-call | tf_op jit(solution)/shard_map/to_owners/pallas_call | solution.py:455
  73.3 0.7 copy.12

commit v4 on v3

v4 whole, which is shorter than its diff:
```python
import functools
import math

import jax
import jax.numpy as jnp
from jax import lax
from jax.experimental import pallas as pl
from jax.experimental.pallas import tpu as pltpu
from jax.sharding import PartitionSpec as P

regular_sq = 0.0025
inv_reg = 1.0 / math.sqrt(regular_sq)
stokes_scale = inv_reg / (8.0 * math.pi)
MESH = pl.DeviceIdType.MESH
VMEM = pl.BlockSpec(memory_space=pltpu.VMEM)
SMEM = pl.BlockSpec(memory_space=pltpu.SMEM)


HBM = pl.BlockSpec(memory_space=pltpu.HBM)
unroll = 16
f32, bf16, ints = jnp.float32, jnp.bfloat16, jnp.int32


def keep(x):
    return pltpu.with_memory_space_constraint(x, pltpu.VMEM)


def far_off(x):
    return pltpu.with_memory_space_constraint(x, pltpu.HBM)


def split3(x):
    high = x.astype(bf16).astype(f32)
    rest = x - high
    middle = rest.astype(bf16).astype(f32)
    return high, middle, rest - middle


def as_row(column):
    return jnp.transpose(jnp.broadcast_to(column, (column.shape[0], 128)))[0:1]


def gather_kernel(
        nrow, ncol, cap, pos_in, nrm_in, curv_in, nct_in, dct_in, own_in, tgt_in, src_in, count_ref,
        near_ref, far_ref, tl_ref, sl_ref, lc_ref, slot_ref, place_ref, cnt_ref,
        nrm_ref, curv_ref, nct_ref, dct_ref, own_ref, tgt_ref, src_ref, here_sem, mine_ref, lists_ref, t_ref, s_ref,
        zsend, zrecv, fsend, frecv, osend, orecv, tsend, trecv, bsend, brecv, xsend, xrecv, gsend, grecv, lsend, lrecv, hsend, hrecv):
    row, col = lax.axis_index("row"), lax.axis_index("col")
    core = lax.rem(col, 2)
    chip = col // 2
    half = ncol // 2
    part = nrow // 2
    i, j = row // part, lax.rem(row, part)
    me = row * ncol + col
    local = pos_in.shape[1]
    drops = own_ref.shape[1]
    per_drop = dct_ref.shape[0]
    slots = tgt_in.shape[1]
    pos_ref = s_ref.at[core, j, 0:3]
    loads = [pltpu.make_async_copy(src, dst, here_sem.at[n]) for n, (src, dst) in enumerate((
        (pos_in, pos_ref), (tgt_in, tgt_ref), (src_in, src_ref), (dct_in, dct_ref), (nct_in, nct_ref), (own_in, own_ref),
        (curv_in, curv_ref), (nrm_in, nrm_ref)))]
    for load in loads:
        load.start()
    barrier = pltpu.get_barrier_semaphore()
    for d in range(1, nrow):
        pl.semaphore_signal(barrier, inc=1, device_id={"row": lax.rem(row + d, nrow)}, device_id_type=MESH)
    for d in range(1, ncol):
        pl.semaphore_signal(barrier, inc=1, device_id={"col": lax.rem(col + d, ncol)}, device_id_type=MESH)

    def remote(src, dst, send, recv, where):
        return pltpu.make_async_remote_copy(
            src_ref=src, dst_ref=dst, send_sem=send, recv_sem=recv, device_id=where, device_id_type=MESH)

    sibling = {"col": col + 1 - 2 * core}

    def along(d, k):
        piece = s_ref.at[core, j, k]
        return remote(piece, piece, zsend.at[d - 1, k], zrecv.at[d - 1, k], {"row": i * part + lax.rem(j + d, part)})

    def source(d):
        return lax.rem(j + part - d, part)

    def onward(d, k):
        piece = s_ref.at[core, source(d), k]
        return remote(piece, piece, fsend.at[d - 1, k], frecv.at[d - 1, k], sibling)

    def own(k):
        piece = s_ref.at[core, j, k]
        return remote(piece, piece, osend.at[k], orecv.at[k], sibling)

    mirror = nrow - 1 - row
    mirror_j = part - 1 - j
    gives = (2 * mirror_j) // part == i
    takes = (2 * j) // part != i

    def index_given(a):
        return jnp.clip(2 * mirror_j + a - i * part, 0, part - 1)

    def index_held(a):
        return jnp.clip(2 * j + a - i * part, 0, part - 1)

    def give(a, k):
        return remote(
            s_ref.at[core, index_given(a), k], t_ref.at[a, col, k], tsend.at[a, k], trecv.at[a, k], {"row": mirror})

    def beside(a):
        piece = t_ref.at[a, col]
        return remote(piece, piece, bsend.at[a], brecv.at[a], sibling)

    def facing(d):
        return 2 * lax.rem(chip + d, half) + core

    def opposite(a, d):
        piece = t_ref.at[a, col]
        return remote(piece, piece, xsend.at[d - 1, a], xrecv.at[d - 1, a], {"col": facing(d)})

    def behind(d):
        return 2 * lax.rem(chip + half - d, half) + core

    def passed(a, d):
        piece = t_ref.at[a, behind(d)]
        return remote(piece, piece, gsend.at[d - 1, a], grecv.at[d - 1, a], sibling)

    def share(a):
        beside(a).start()
        for d in range(1, half):
            opposite(a, d).start()

    def on_positions(index, k):
        for a in range(2):
            @pl.when(gives & (index_given(a) == index))
            def _():
                give(a, k).start()

            @pl.when(jnp.logical_not(takes) & (index_held(a) == index))
            def _():
                t_ref[a, col, k] = s_ref[core, index, k]
                if k == 2:
                    share(a)

    def list_to(e):
        return remote(
            mine_ref, lists_ref.at[lax.rem(row, 2), core], lsend.at[e], lrecv.at[lax.rem(row, 2)], {"row": e * part + row // 2})

    def list_on(a):
        piece = lists_ref.at[a, core]
        return remote(piece, piece, hsend.at[a], hrecv.at[a], sibling)

    loads[0].wait()
    pl.semaphore_wait(barrier, nrow + ncol - 2)
    for k in range(3):
        for d in range(1, part):
            along(d, k).start()
    for k in range(3):
        on_positions(j, k)
    for load in loads[1:]:
        load.wait()
    zero = jnp.zeros((1, slots), ints)
    mine_ref[...] = jnp.concatenate(
        [tgt_ref[...], src_ref[...], jnp.full((1, slots), count_ref[0], ints), zero, zero, zero, zero, zero], axis=0)
    for e in range(2):
        @pl.when(e * part + row // 2 != row)
        def _():
            list_to(e).start()

        @pl.when(e * part + row // 2 == row)
        def _():
            lists_ref[lax.rem(row, 2), core] = mine_ref[...]

    index = lax.broadcasted_iota(ints, (local, 1), 0)
    ids = me * local + index
    home = (2 * j + i) * ncol + col
    home_ids = home * local + index

    def match(chunk, carry):
        counts, owners = carry
        lanes = pl.ds(pl.multiple_of(chunk * 128, 128), 128)
        clusters, nodes_in, owner = dct_ref[:, lanes], nct_ref[:, lanes], own_ref[0:1, lanes]
        for k in range(per_drop):
            counts = counts + jnp.where(ids == clusters[k:k + 1], nodes_in[k:k + 1], 0)
            owners = owners + jnp.where(home_ids == clusters[k:k + 1], owner, 0)
        return counts, owners

    none = jnp.zeros((local, 128), ints)
    counts, owners = lax.fori_loop(0, drops // 128, match, (none, none))
    home_counts = jnp.sum(counts, axis=1, keepdims=True, dtype=ints)
    home_owner = jnp.sum(owners, axis=1, keepdims=True, dtype=ints)
    scale = jnp.where(lax.broadcasted_iota(ints, (local, 128), 1) < home_counts, curv_ref[...], 0.0)
    for k in range(3):
        s_ref[core, j, 3 + k] = scale * nrm_ref[k]
        for d in range(1, part):
            along(d, 3 + k).start()
    for k in range(6):
        own(k).start()

    def spread(l, r, k):
        at = (l * part + r) * local * 8 + (k if k < 3 else k + 1)
        far_ref[pl.ds(at, local, stride=8), :] = s_ref[l, r, k]

    def blank(l, r):
        for k in (3, 7):
            far_ref[pl.ds((l * part + r) * local * 8 + k, local, stride=8), :] = jnp.zeros((local, 128), f32)

    def arrive(k):
        for d in range(1, part):
            along(d, k).wait_recv()
            onward(d, k).start()
            if k < 3:
                on_positions(source(d), k)

    def targets(a, c):
        square = jnp.ones((local, 128), f32)
        start = (a * ncol + c) * local * 8
        for k in range(3):
            coord = t_ref[a, c, k]
            centre = jnp.mean(coord, axis=1, keepdims=True)
            coord = (coord - centre) * inv_reg
            square = square + coord * coord
            near_ref[pl.ds(start + k, local, stride=8), :] = coord
            near_ref[pl.ds(start + 4 + k, local, stride=8), :] = jnp.broadcast_to(centre, coord.shape)
        near_ref[pl.ds(start + 3, local, stride=8), :] = square
        near_ref[pl.ds(start + 7, local, stride=8), :] = jnp.zeros((local, 128), f32)

    for k in range(3):
        arrive(k)
    for a in range(2):
        @pl.when(2 * j + a != row)
        def _():
            remote(mine_ref, lists_ref.at[a, core], lsend.at[0], lrecv.at[a], sibling).wait_recv()

        list_on(a).start()

    owner_row = as_row(home_owner.astype(f32)).astype(ints)
    lane = lax.broadcasted_iota(ints, (local, local), 1)
    rank = jnp.sum(((owner_row == home_owner) & (lane < index)).astype(ints), axis=1, keepdims=True, dtype=ints)
    slot_ref[...] = as_row((home_owner * cap + rank).astype(f32)).astype(ints)
    drop_of = lax.div(index, per_drop)
    width = 256 if drops % 256 == 0 else 128
    before = (lax.broadcasted_iota(ints, (width, width), 0) < lax.broadcasted_iota(ints, (width, width), 1)).astype(bf16)

    def owned(chunk, carry):
        clusters, counted, base = carry
        lanes = pl.ds(pl.multiple_of(chunk * width, width), width)
        mine = own_ref[0:1, lanes] == me
        marks = jnp.broadcast_to(mine.astype(f32), (16, width)).astype(bf16)
        place = jnp.dot(marks, before, preferred_element_type=f32)[0:1].astype(ints) + base
        chosen = mine & (place == drop_of)
        clusters = clusters + jnp.where(chosen, jnp.concatenate([dct_ref[:, lanes]] * (local // per_drop), axis=0), 0)
        counted = counted + jnp.where(chosen, jnp.concatenate([nct_ref[:, lanes]] * (local // per_drop), axis=0), 0)
        return clusters, counted, base + jnp.sum(mine.astype(ints), axis=1, keepdims=True, dtype=ints)

    wide = jnp.zeros((local, width), ints)
    clusters, counted, _ = lax.fori_loop(0, drops // width, owned, (wide, wide, jnp.zeros((1, 1), ints)))
    clusters = jnp.sum(clusters, axis=1, keepdims=True, dtype=ints)
    cnt_ref[...] = jnp.sum(counted, axis=1, keepdims=True, dtype=ints)
    clusters_row = as_row(clusters.astype(f32)).astype(ints)
    anchor, anchor_row = lax.div(clusters, local), lax.div(clusters_row, local)
    same = (anchor == anchor_row) & (clusters_row < clusters)
    home_row, home_col = lax.div(anchor, ncol), lax.rem(anchor, ncol)
    keeper = (lax.rem(home_row, 2) * part + lax.div(home_row, 2)) * ncol + home_col
    place_ref[...] = keeper * cap + jnp.sum(same.astype(ints), axis=1, keepdims=True, dtype=ints)

    @pl.when(takes)
    def _():
        for a in range(2):
            for k in range(3):
                give(a, k).wait_recv()
            share(a)

    for k in range(6):
        spread(core, j, k)
    for l in range(2):
        for r in range(part):
            blank(l, r)
    for a in range(2):
        targets(a, col)

    for a in range(2):
        list_on(a).wait_recv()
    lane_of = lax.broadcasted_iota(ints, (1, slots), 1)
    lowest = i * part * local
    square_rows = lax.broadcasted_iota(ints, (slots, slots), 0)
    earlier = (square_rows < lax.broadcasted_iota(ints, (slots, slots), 1)).astype(f32).astype(bf16)
    for a in range(2):
        for l in range(2):
            t, s, count = lists_ref[a, l, 0:1, :], lists_ref[a, l, 1:2, :], lists_ref[a, l, 2:3, :]
            taken = (lane_of < count) & (s >= lowest) & (s < lowest + part * local)
            marks = taken.astype(f32)
            ranks = jnp.dot(jnp.broadcast_to(marks, (16, slots)).astype(bf16), earlier, preferred_element_type=f32)[0:1]
            ranks = jnp.where(taken, ranks.astype(ints), -1)
            to = (square_rows == ranks).astype(f32).astype(bf16)
            digits = [lax.div(t, 256), lax.rem(t, 256), lax.div(s, 256), lax.rem(s, 256)]
            values = jnp.concatenate([v.astype(f32) for v in digits] + [jnp.zeros((12, slots), f32)], axis=0).astype(bf16)
            moved = lax.dot_general(values, to, (((1,), (1,)), ((), ())), preferred_element_type=f32).astype(ints)
            n = a * 2 + l
            tl_ref[n:n + 1, :] = moved[0:1] * 256 + moved[1:2] + a * ncol * local
            sl_ref[n:n + 1, :] = jnp.maximum(moved[2:3] * 256 + moved[3:4] - lowest, 0) + l * part * local
            lc_ref[n:n + 1, :] = jnp.broadcast_to(jnp.sum(marks, axis=1, keepdims=True).astype(ints), (1, 128))

    for a in range(2):
        for d in range(1, half):
            opposite(a, d).wait_recv()
            passed(a, d).start()
        beside(a).wait_recv()
        targets(a, col + 1 - 2 * core)
        for d in range(1, half):
            targets(a, behind(d))
    for k in range(3, 6):
        arrive(k)
    for k in range(6):
        own(k).wait_recv()
        spread(1 - core, j, k)
        for d in range(1, part):
            spread(core, source(d), k)
    for a in range(2):
        for d in range(1, half):
            passed(a, d).wait_recv()
            targets(a, behind(d) + 1 - 2 * core)
    for k in range(6):
        for d in range(1, part):
            onward(d, k).wait_recv()
            spread(1 - core, source(d), k)
    for k in range(6):
        own(k).wait_send()
        for d in range(1, part):
            along(d, k).wait_send()
            onward(d, k).wait_send()
    for a in range(2):
        @pl.when(gives)
        def _():
            for k in range(3):
                give(a, k).wait_send()

        beside(a).wait_send()
        list_on(a).wait_send()
        for d in range(1, half):
            opposite(a, d).wait_send()
            passed(a, d).wait_send()
    for e in range(2):
        @pl.when(e * part + row // 2 != row)
        def _():
            list_to(e).wait_send()


def pair_kernel(tl_ref, sl_ref, lc_ref, near_ref, far_ref, v_ref, acc_ref, both_a, both_b, g_a, g_b):
    _, ncol, _, local, _ = v_ref.shape
    core = lax.rem(lax.axis_index("col"), 2)
    sub = lax.broadcasted_iota(ints, (8, 128), 0)
    low = sub < 4
    last = (sub == 3) | (sub == 7)
    scale = jnp.where(low, -2.0, 1.0).astype(f32)
    fold = jnp.where(sub == 3, 1.0, jnp.where(sub == 7, -1.0, 0.0)).astype(f32)
    some = jnp.where(low, 1.0, 0.0).astype(f32)
    unit = jnp.where(low, inv_reg, 1.0).astype(f32)
    idle = jnp.where(low, inv_reg, 0.0).astype(f32)
    nothing = jnp.zeros((32, 128), bf16)
    acc_ref[...] = jnp.zeros_like(acc_ref)
    both_b[...] = jnp.ones_like(both_b)
    g_b[...] = jnp.zeros_like(g_b)
    ends = [lc_ref[0, 0]]
    for l in range(1, 4):
        ends.append(ends[-1] + lc_ref[l, 0])
    total = ends[3]
    half = (total + 1) // 2
    first = core * half
    n = jnp.where(core == 0, half, total - half)

    def entry(j):
        j = jnp.minimum(first + jnp.clip(j, 0, jnp.maximum(n - 1, 0)), jnp.maximum(total - 1, 0))
        past = [(j >= end).astype(ints) for end in ends[:3]]
        start = jnp.where(j >= ends[2], ends[2], jnp.where(j >= ends[1], ends[1], jnp.where(j >= ends[0], ends[0], 0)))
        return past[0] + past[1] + past[2], j - start

    def tile(i):
        return pl.ds(pl.multiple_of(i * 8, 8), 8)

    def distances(block, both_ref, g_ref):
        for u in range(unroll):
            j = block * unroll + u
            l, e = entry(j)
            t, s = tl_ref[l, e], sl_ref[l, e]
            near = near_ref[tile(t), :]
            centre = jnp.where(low, pltpu.roll(near, 4, 0), 0.0)
            high, middle, rest = split3(near)
            sums = jnp.where(sub == 0, high[3:4], jnp.where(sub == 1, middle[3:4], jnp.where(sub == 2, rest[3:4], 0.0)))
            high = jnp.where(sub < 3, high, jnp.where(sub == 3, 1.0, 0.0))
            middle = jnp.where(sub < 3, middle, 0.0)
            rest = jnp.where(sub < 3, rest, 0.0)
            high_up = pltpu.roll(high, 4, 0)
            right = jnp.concatenate([
                high + pltpu.roll(middle, 4, 0), rest + high_up, middle + high_up, sums], axis=0).astype(bf16)
            shifted = (far_ref[tile(s), :] - centre) * jnp.where(j < n, unit, idle)
            prod = shifted * jnp.where(low, shifted, pltpu.roll(shifted, 4, 0))
            prod = prod + pltpu.roll(prod, 1, 0)
            prod = prod + pltpu.roll(prod, 2, 0)
            hi, mid, lo = split3(shifted * scale + prod * fold)
            hi_up, mid_up, lo_up = pltpu.roll(hi, 4, 0), pltpu.roll(mid, 4, 0), pltpu.roll(lo, 4, 0)
            left = jnp.concatenate([
                jnp.where(low, hi, hi_up), jnp.where(low, hi, mid_up), jnp.where(low, mid, lo_up), some,
                jnp.where(low, hi_up, hi), jnp.where(low, hi_up, mid), jnp.where(low, mid_up, lo),
                jnp.zeros((8, 128), f32)], axis=0).astype(bf16)
            weights = jnp.concatenate([
                jnp.concatenate([right, nothing], axis=1), jnp.concatenate([nothing, right], axis=1)], axis=0)
            both_ref[u] = lax.dot_general(left, weights, (((0,), (0,)), ((), ())), preferred_element_type=f32)
            g_ref[u] = jnp.concatenate([jnp.where(last, 1.0, hi), jnp.where(last, 0.0, mid)], axis=0).astype(bf16)

    def speeds(block, both_ref, g_ref):
        for u in range(unroll):
            l, e = entry(block * unroll + u)
            t = tl_ref[l, e]
            both, g = both_ref[u], g_ref[u]
            inv = lax.rsqrt(both[:, 0:128])
            weight = inv * inv * inv
            iso = inv + weight
            pro = both[:, 128:256] * weight
            iso_hi, pro_hi = iso.astype(bf16), pro.astype(bf16)
            iso_lo = (iso - iso_hi.astype(f32)).astype(bf16)
            pro_lo = (pro - pro_hi.astype(f32)).astype(bf16)
            m = jnp.concatenate([
                jnp.concatenate([iso_hi, pro_hi], axis=1), jnp.concatenate([iso_lo, pro_lo], axis=1)], axis=0)
            out = jnp.dot(jnp.concatenate([g, g], axis=1), m, preferred_element_type=f32)
            out = out[0:8] + out[8:16]
            from_iso, from_pro = out[:, 0:128], out[:, 128:256]
            acc_ref[tile(t), :] += pltpu.roll(from_iso, 4, 0) + near_ref[tile(t), :] * from_pro[3:4] + 0.5 * from_pro

    def many(i, carry):
        distances(2 * i, both_a, g_a)
        speeds(2 * i - 1, both_b, g_b)
        distances(2 * i + 1, both_b, g_b)
        speeds(2 * i, both_a, g_a)
        return carry

    lax.fori_loop(0, (n + unroll - 1) // unroll // 2 + 1, many, 0)
    for a in range(2):
        for c in range(ncol):
            for k in range(3):
                v_ref[a, c, k] = stokes_scale * acc_ref[pl.ds((a * ncol + c) * local * 8 + k, local, stride=8), :]


def home_kernel(
        nrow, ncol, cap, slot_ref, place_ref, cnt_ref, v_ref, out_ref, got, part, swap, outg, arr, vsend, vrecv, zsend, zrecv, asend, arecv):
    row, col = lax.axis_index("row"), lax.axis_index("col")
    local = out_ref.shape[1]
    devs = nrow * ncol
    me = row * ncol + col
    barrier = pltpu.get_barrier_semaphore()

    def peer(d):
        p = lax.rem(me + d, devs)
        return {"row": p // ncol, "col": lax.rem(p, ncol)}

    for d in range(1, devs):
        pl.semaphore_signal(barrier, inc=1, device_id=peer(d), device_id_type=MESH)
    half = ncol // 2
    core = lax.rem(col, 2)
    mine_x = col // 2

    def remote(src, dst, send, recv, where):
        return pltpu.make_async_remote_copy(
            src_ref=src, dst_ref=dst, send_sem=send, recv_sem=recv, device_id=where, device_id_type=MESH)

    rows = nrow // 2
    keep_a = row // rows
    order = (1 - keep_a, keep_a)

    def within(n, d, k):
        x = lax.rem(mine_x + d, half)
        return remote(
            v_ref.at[order[n], 2 * x + 1 - core, k], got.at[n, d, k], vsend.at[n, d, k], vrecv.at[n, d, k],
            {"col": col + 1 - 2 * core})

    def facing(d):
        return 2 * lax.rem(mine_x + d, half) + core

    def across(n, d, k):
        at = half + d - 1
        return remote(
            part.at[n, d - 1, k], got.at[n, at, k], vsend.at[n, at, k], vrecv.at[n, at, k], {"col": facing(d)})

    def exchange(k):
        return remote(swap.at[0, k], swap.at[1, k], zsend.at[k], zrecv.at[k], {"row": lax.rem(row + rows, nrow)})

    def total(n, k):
        within(n, 0, k).wait_recv()
        mine = v_ref[order[n], col, k] + got[n, 0, k]
        for d in range(1, half):
            across(n, d, k).wait_recv()
            mine = mine + got[n, half + d - 1, k]
        return mine

    def deal(d, k):
        return remote(outg.at[k, lax.rem(me + d, devs)], arr.at[k, me], asend.at[d - 1, k], arecv.at[d - 1, k], peer(d))

    def move(pick, values):
        parts = jnp.concatenate(split3(values), axis=1).astype(bf16)
        moved = jnp.dot(pick, parts, preferred_element_type=f32)
        return moved[:, 0:128] + moved[:, 128:256] + moved[:, 256:384]

    pick = (lax.broadcasted_iota(ints, (devs * cap, local), 0) == slot_ref[...]).astype(f32).astype(bf16)
    pl.semaphore_wait(barrier, devs - 1)
    for n in range(2):
        for k in range(3):
            for d in [*range(1, half), 0]:
                within(n, d, k).start()

    def pass_on(n, k):
        for d in range(1, half):
            within(n, d, k).wait_recv()
            part[n, d - 1, k] = v_ref[order[n], facing(d), k] + got[n, d, k]
            across(n, d, k).start()

    for k in range(3):
        pass_on(0, k)
    for k in range(3):
        swap[0, k] = total(0, k)
        exchange(k).start()
        pass_on(1, k)
    for k in range(3):
        mine = total(1, k)
        exchange(k).wait_recv()
        outg[k] = move(pick, mine + swap[1, k]).reshape(devs, cap, 128)
        for d in range(1, devs):
            deal(d, k).start()
        arr[k, me] = outg[k, me]
    fetch = (lax.broadcasted_iota(ints, (local, devs * cap), 1) == place_ref[...]).astype(f32).astype(bf16)
    live = lax.broadcasted_iota(ints, (local, 128), 1) < cnt_ref[...]
    for k in range(3):
        for d in range(1, devs):
            deal(d, k).wait_recv()
        out_ref[k] = jnp.where(live, move(fetch, arr[k].reshape(devs * cap, 128)), 0.0)
    for k in range(3):
        exchange(k).wait_send()
        for n in range(2):
            for d in range(half):
                within(n, d, k).wait_send()
            for d in range(1, half):
                across(n, d, k).wait_send()
        for d in range(1, devs):
            deal(d, k).wait_send()


def per_device(positions, normals, curvature, pair_targets, pair_sources, pair_count, node_counts, drop_clusters, drop_owner):
    local, _, nodes = positions.shape
    nrow, ncol = lax.axis_size("row"), lax.axis_size("col")
    devs = nrow * ncol
    part, half = nrow // 2, ncol // 2
    cap = max(2, 2 * local // devs)
    slots = pair_targets.shape[1]
    dma = pltpu.SemaphoreType.DMA
    shape = jax.ShapeDtypeStruct
    near, far, tl, sl, lc, slot, place, owned_counts = pl.pallas_call(
        functools.partial(gather_kernel, nrow, ncol, cap),
        out_shape=(
            pltpu.VMEM((2 * ncol * local * 8, nodes), f32), pltpu.VMEM((2 * part * local * 8, nodes), f32),
            shape((4, slots), ints), shape((4, slots), ints), shape((4, 128), ints),
            pltpu.VMEM((1, local), ints), pltpu.VMEM((local, 1), ints), pltpu.VMEM((local, 1), ints)),
        in_specs=[HBM] * 8 + [SMEM], out_specs=(VMEM,) * 8,
        scratch_shapes=[
            pltpu.VMEM((3, local, nodes), f32), pltpu.VMEM((local, nodes), f32), *[pltpu.VMEM(drop_clusters.shape[::-1], ints)] * 2,
            pltpu.VMEM((1, drop_owner.shape[0]), ints), *[pltpu.VMEM((1, slots), ints)] * 2, dma((8,)),
            pltpu.VMEM((8, slots), ints), pltpu.VMEM((2, 2, 8, slots), ints),
            pltpu.VMEM((2, ncol, 3, local, nodes), f32), pltpu.VMEM((2, part, 6, local, nodes), f32),
            *[dma((part - 1, 6))] * 4, *[dma((6,))] * 2, *[dma((2, 3))] * 2, *[dma((2,))] * 2,
            *[dma((max(half - 1, 1), 2))] * 4, *[dma((2,))] * 4],
        compiler_params=pltpu.CompilerParams(collective_id=0, has_side_effects=True, vmem_limit_bytes=30 << 20),
        name="gather_blocks",
    )(*map(far_off, (jnp.transpose(positions, (1, 0, 2)), jnp.transpose(normals, (1, 0, 2)), curvature, node_counts.T,
                     drop_clusters.T, drop_owner[None, :], pair_targets, pair_sources)), pair_count)
    speeds = pl.pallas_call(
        pair_kernel,
        out_shape=pltpu.VMEM((2, ncol, 3, local, nodes), f32),
        in_specs=[SMEM] * 3 + [VMEM] * 2, out_specs=VMEM,
        scratch_shapes=[pltpu.VMEM((2 * ncol * local * 8, nodes), f32)]
        + [pltpu.VMEM((unroll, nodes, 2 * nodes), f32)] * 2 + [pltpu.VMEM((unroll, 16, nodes), bf16)] * 2,
        compiler_params=pltpu.CompilerParams(vmem_limit_bytes=30 << 20),
        name="pairs",
    )(tl, sl, lc, keep(near), keep(far))
    owned = pl.pallas_call(
        functools.partial(home_kernel, nrow, ncol, cap),
        out_shape=jax.ShapeDtypeStruct((3, local, nodes), f32),
        in_specs=[VMEM] * 4, out_specs=VMEM,
        scratch_shapes=[
            pltpu.VMEM((2, ncol - 1, 3, local, nodes), f32), pltpu.VMEM((2, max(half - 1, 1), 3, local, nodes), f32),
            pltpu.VMEM((2, 3, local, nodes), f32),
            pltpu.VMEM((3, devs, cap, nodes), f32), pltpu.VMEM((3, devs, cap, nodes), f32),
            dma((2, ncol - 1, 3)), dma((2, ncol - 1, 3)), dma((3,)), dma((3,)), dma((devs - 1, 3)), dma((devs - 1, 3)),
        ],
        compiler_params=pltpu.CompilerParams(collective_id=1, has_side_effects=True, vmem_limit_bytes=30 << 20),
        name="to_owners",
    )(keep(slot), keep(place), keep(owned_counts), keep(speeds))
    return jnp.transpose(owned, (1, 0, 2))


def solution(mesh):
    every = ("groups", "row", "col")
    in_specs = (
        P(every, None, None), P(every, None, None), P(every, None), P(every, None), P(every, None), P(every),
        P("groups", None), P("groups", None), P("groups"),
    )
    return jax.shard_map(per_device, mesh=mesh, in_specs=in_specs, out_specs=P(every, None, None), check_vma=False)
```

time: 73.4 us -> 69.4 us (0.946)
  Pallas kernels: 72.6 us -> 68.2 us
    pallas_call x1, Pallas kernels: 35.1 us -> 18.6 us  [per_device(): pl.pallas_call(functools.partial(gather_kernel, nrow, ncol, cap), out_sha...]
    pallas_call x1, Pallas kernels: 25 us -> 36.4 us  [per_device(): pl.pallas_call(functools.partial(home_kernel, nrow, ncol, cap), out_shape...]
where the time goes in v4:
time: 69.4 us; the launch traced here: 69.5 us
  Pallas kernels  68.2 us (98%)
    pallas_call x1, Pallas kernels, per_device(): pl.pallas_call(functools.partial(home_kernel, nrow, ncol, cap), out_shape...  36.4 us
    pallas_call x1, Pallas kernels, per_device(): pl.pallas_call(functools.partial(gather_kernel, nrow, ncol, cap), out_sha...  18.6 us
    pallas_call x1, Pallas kernels, per_device(): pl.pallas_call(pair_kernel, out_shape=pltpu.VMEM((2, ncol, 3, local, node...  13.2 us

profile of v4, /device:TPU:0, one launch (start us, length us, event | category | flops | bytes accessed | tf_op | source)
XLA Modules:
  0.0 69.5 jit_solution(8607751856444312806)
XLA Ops:
  0.7 18.6 %gather_blocks.1 = (f32[8192,128]{1,0:T(8,128)S(1)}, f32[4096,128]{1,0:T(8,128)S(1)}, s32[4,512]{1,0:T(4,128)S(1)}, s32[4,512]{1,0:T(4,128)S(1)}, s32[4,128]{1,0...) custom-call(f32[3,128,128]{2,1,0:T(8,128)} %bitcast.7, f32[3,128,128]{2,1,0:T(8,128)} %bitcast.8, ...), custom_call_target="tpu_custom_call" | custom-call | tf_op jit(solution)/shard_map/gather_blocks/pallas_call | solution.py:552
  19.3 13.2 %pairs.1.v_ref = f32[2,4,3,128,128]{4,3,2,1,0:T(8,128)S(1)} custom-call(s32[4,512]{1,0:T(4,128)S(1)} %get-tuple-element.16.tl_ref, s32[4,512]{1,0:T(4,128)S(1)} %get-tuple-element.17.sl_ref, s32[4,128]{1,0:T(4,128)S(1)} %get-tuple-element.18.lc_ref, f32[8192,128]{1,0:T(8,128)S(1)} %get-tuple-element.19.near_ref, f32[4096,128]{1,0:T(8,128)S(1)} %get-tuple-element.20.far_ref), custom_call_target="tpu_custom_call" | custom-call | tf_op jit(solution)/shard_map/pairs/pallas_call | solution.py:570
  32.4 36.4 %to_owners.1 = f32[3,128,128]{2,1,0:T(8,128)S(1)} custom-call(s32[1,128]{1,0:T(1,128)S(1)} %get-tuple-element.13.slot_ref, s32[128,1]{1,0:T(8,128)S(1)} %get-tuple-element.14.place_ref, s32[128,1]{1,0:T(8,128)S(1)} %get-tuple-element.15.cnt_ref, f32[2,4,3,128,128]{4,3,2,1,0:T(8,128)S(1)} %pairs.1.v_ref), custom_call_target="tpu_custom_call" | custom-call | tf_op jit(solution)/shard_map/to_owners/pallas_call | solution.py:579
  68.9 0.7 copy.12

commit v5 on v4

--- a/solution.py
+++ b/solution.py
@@ -44,19 +44,21 @@
         nrow, ncol, cap, pos_in, nrm_in, curv_in, nct_in, dct_in, own_in, tgt_in, src_in, count_ref,
         near_ref, far_ref, tl_ref, sl_ref, lc_ref, slot_ref, place_ref, cnt_ref,
         nrm_ref, curv_ref, nct_ref, dct_ref, own_ref, tgt_ref, src_ref, here_sem, mine_ref, lists_ref, t_ref, s_ref,
-        zsend, zrecv, fsend, frecv, osend, orecv, tsend, trecv, bsend, brecv, xsend, xrecv, gsend, grecv, lsend, lrecv, hsend, hrecv):
+        zsend, zrecv, fsend, frecv, osend, orecv, bsend, brecv, xsend, xrecv, gsend, grecv, lsend, lrecv, hsend, hrecv):
     row, col = lax.axis_index("row"), lax.axis_index("col")
     core = lax.rem(col, 2)
     chip = col // 2
     half = ncol // 2
     part = nrow // 2
-    i, j = row // part, lax.rem(row, part)
+    i = lax.rem(row, 2)
+    mate = row + 1 - 2 * i
+    based = row // part == i
     me = row * ncol + col
     local = pos_in.shape[1]
     drops = own_ref.shape[1]
     per_drop = dct_ref.shape[0]
     slots = tgt_in.shape[1]
-    pos_ref = s_ref.at[core, j, 0:3]
+    pos_ref = s_ref.at[core, row, 0:3]
     loads = [pltpu.make_async_copy(src, dst, here_sem.at[n]) for n, (src, dst) in enumerate((
         (pos_in, pos_ref), (tgt_in, tgt_ref), (src_in, src_ref), (dct_in, dct_ref), (nct_in, nct_ref), (own_in, own_ref),
         (curv_in, curv_ref), (nrm_in, nrm_ref)))]
@@ -74,35 +76,41 @@
 
     sibling = {"col": col + 1 - 2 * core}
 
-    def along(d, k):
-        piece = s_ref.at[core, j, k]
-        return remote(piece, piece, zsend.at[d - 1, k], zrecv.at[d - 1, k], {"row": i * part + lax.rem(j + d, part)})
-
-    def source(d):
-        return lax.rem(j + part - d, part)
-
-    def onward(d, k):
-        piece = s_ref.at[core, source(d), k]
-        return remote(piece, piece, fsend.at[d - 1, k], frecv.at[d - 1, k], sibling)
+    def block_of(way, step):
+        return jnp.clip(row - way * step, 0, nrow - 1)
+
+    def relay(way, step, k):
+        piece = s_ref.at[core, block_of(way, step), k]
+        at = step if way > 0 else nrow - 1 + step
+        return remote(piece, piece, zsend.at[at, k], zrecv.at[at, k], {"row": jnp.clip(row + way, 0, nrow - 1)})
+
+    def reaches(way, block, place):
+        inside = (block >= 0) & (block < nrow)
+        half_of = jnp.clip(block, 0, nrow - 1) // part
+        return inside & (place <= nrow - 2 + half_of if way > 0 else place >= half_of)
+
+    def sends(way, step):
+        return reaches(way, row - way * step, row + way)
+
+    def receives(way, step):
+        return reaches(way, row - way * (step + 1), row)
+
+    def wanted(way, step):
+        return receives(way, step) & (block_of(way, step + 1) // part == i)
+
+    def onward(way, step, k):
+        piece = s_ref.at[core, block_of(way, step + 1), k]
+        at = step if way > 0 else nrow - 1 + step
+        return remote(piece, piece, fsend.at[at, k], frecv.at[at, k], sibling)
+
+    def start(way, step, k):
+        @pl.when(sends(way, step))
+        def _():
+            relay(way, step, k).start()
 
     def own(k):
-        piece = s_ref.at[core, j, k]
+        piece = s_ref.at[core, row, k]
         return remote(piece, piece, osend.at[k], orecv.at[k], sibling)
-
-    mirror = nrow - 1 - row
-    mirror_j = part - 1 - j
-    gives = (2 * mirror_j) // part == i
-    takes = (2 * j) // part != i
-
-    def index_given(a):
-        return jnp.clip(2 * mirror_j + a - i * part, 0, part - 1)
-
-    def index_held(a):
-        return jnp.clip(2 * j + a - i * part, 0, part - 1)
-
-    def give(a, k):
-        return remote(
-            s_ref.at[core, index_given(a), k], t_ref.at[a, col, k], tsend.at[a, k], trecv.at[a, k], {"row": mirror})
 
     def beside(a):
         piece = t_ref.at[a, col]
@@ -127,21 +135,8 @@
         for d in range(1, half):
             opposite(a, d).start()
 
-    def on_positions(index, k):
-        for a in range(2):
-            @pl.when(gives & (index_given(a) == index))
-            def _():
-                give(a, k).start()
-
-            @pl.when(jnp.logical_not(takes) & (index_held(a) == index))
-            def _():
-                t_ref[a, col, k] = s_ref[core, index, k]
-                if k == 2:
-                    share(a)
-
-    def list_to(e):
-        return remote(
-            mine_ref, lists_ref.at[lax.rem(row, 2), core], lsend.at[e], lrecv.at[lax.rem(row, 2)], {"row": e * part + row // 2})
+    def list_to(a):
+        return remote(mine_ref, lists_ref.at[a, core], lsend.at[0], lrecv.at[0], {"row": mate})
 
     def list_on(a):
         piece = lists_ref.at[a, core]
@@ -150,36 +145,28 @@
     loads[0].wait()
     pl.semaphore_wait(barrier, nrow + ncol - 2)
     for k in range(3):
-        for d in range(1, part):
-            along(d, k).start()
-    for k in range(3):
-        on_positions(j, k)
+        for way in (1, -1):
+            start(way, 0, k)
+        t_ref[i, col, k] = s_ref[core, row, k]
+    share(i)
     for load in loads[1:]:
         load.wait()
     zero = jnp.zeros((1, slots), ints)
     mine_ref[...] = jnp.concatenate(
         [tgt_ref[...], src_ref[...], jnp.full((1, slots), count_ref[0], ints), zero, zero, zero, zero, zero], axis=0)
-    for e in range(2):
-        @pl.when(e * part + row // 2 != row)
-        def _():
-            list_to(e).start()
-
-        @pl.when(e * part + row // 2 == row)
-        def _():
-            lists_ref[lax.rem(row, 2), core] = mine_ref[...]
-
+    list_to(i).start()
+    lists_ref[i, core] = mine_ref[...]
     index = lax.broadcasted_iota(ints, (local, 1), 0)
     ids = me * local + index
-    home = (2 * j + i) * ncol + col
-    home_ids = home * local + index
 
     def match(chunk, carry):
         counts, owners = carry
         lanes = pl.ds(pl.multiple_of(chunk * 128, 128), 128)
         clusters, nodes_in, owner = dct_ref[:, lanes], nct_ref[:, lanes], own_ref[0:1, lanes]
         for k in range(per_drop):
-            counts = counts + jnp.where(ids == clusters[k:k + 1], nodes_in[k:k + 1], 0)
-            owners = owners + jnp.where(home_ids == clusters[k:k + 1], owner, 0)
+            hit = ids == clusters[k:k + 1]
+            counts = counts + jnp.where(hit, nodes_in[k:k + 1], 0)
+            owners = owners + jnp.where(hit, owner, 0)
         return counts, owners
 
     none = jnp.zeros((local, 128), ints)
@@ -188,26 +175,47 @@
     home_owner = jnp.sum(owners, axis=1, keepdims=True, dtype=ints)
     scale = jnp.where(lax.broadcasted_iota(ints, (local, 128), 1) < home_counts, curv_ref[...], 0.0)
     for k in range(3):
-        s_ref[core, j, 3 + k] = scale * nrm_ref[k]
-        for d in range(1, part):
-            along(d, 3 + k).start()
-    for k in range(6):
-        own(k).start()
-
-    def spread(l, r, k):
-        at = (l * part + r) * local * 8 + (k if k < 3 else k + 1)
-        far_ref[pl.ds(at, local, stride=8), :] = s_ref[l, r, k]
+        s_ref[core, row, 3 + k] = scale * nrm_ref[k]
+        for way in (1, -1):
+            start(way, 0, 3 + k)
+
+    @pl.when(based)
+    def _():
+        for k in range(6):
+            own(k).start()
+
+    def spread(l, block, k):
+        at = (l * part + lax.rem(block, part)) * local * 8 + (k if k < 3 else k + 1)
+        far_ref[pl.ds(at, local, stride=8), :] = s_ref[l, block, k]
 
     def blank(l, r):
         for k in (3, 7):
             far_ref[pl.ds((l * part + r) * local * 8 + k, local, stride=8), :] = jnp.zeros((local, 128), f32)
 
-    def arrive(k):
-        for d in range(1, part):
-            along(d, k).wait_recv()
-            onward(d, k).start()
-            if k < 3:
-                on_positions(source(d), k)
+    def arrive(step, k):
+        for way in (1, -1):
+            @pl.when(receives(way, step))
+            def _():
+                relay(way, step, k).wait_recv()
+                if step < nrow - 2:
+                    start(way, step + 1, k)
+
+                @pl.when(wanted(way, step))
+                def _():
+                    onward(way, step, k).start()
+
+    def collect(step, k):
+        for way in (1, -1):
+            @pl.when(wanted(way, step))
+            def _():
+                spread(core, block_of(way, step + 1), k)
+
+    def received(step, k):
+        for way in (1, -1):
+            @pl.when(wanted(way, step))
+            def _():
+                onward(way, step, k).wait_recv()
+                spread(1 - core, block_of(way, step + 1), k)
 
     def targets(a, c):
         square = jnp.ones((local, 128), f32)
@@ -223,12 +231,11 @@
         near_ref[pl.ds(start + 7, local, stride=8), :] = jnp.zeros((local, 128), f32)
 
     for k in range(3):
-        arrive(k)
-    for a in range(2):
-        @pl.when(2 * j + a != row)
-        def _():
-            remote(mine_ref, lists_ref.at[a, core], lsend.at[0], lrecv.at[a], sibling).wait_recv()
-
+        arrive(0, k)
+        t_ref[1 - i, col, k] = s_ref[core, mate, k]
+    share(1 - i)
+    list_to(1 - i).wait_recv()
+    for a in range(2):
         list_on(a).start()
 
     owner_row = as_row(home_owner.astype(f32)).astype(ints)
@@ -257,19 +264,10 @@
     clusters_row = as_row(clusters.astype(f32)).astype(ints)
     anchor, anchor_row = lax.div(clusters, local), lax.div(clusters_row, local)
     same = (anchor == anchor_row) & (clusters_row < clusters)
-    home_row, home_col = lax.div(anchor, ncol), lax.rem(anchor, ncol)
-    keeper = (lax.rem(home_row, 2) * part + lax.div(home_row, 2)) * ncol + home_col
-    place_ref[...] = keeper * cap + jnp.sum(same.astype(ints), axis=1, keepdims=True, dtype=ints)
-
-    @pl.when(takes)
-    def _():
-        for a in range(2):
-            for k in range(3):
-                give(a, k).wait_recv()
-            share(a)
-
-    for k in range(6):
-        spread(core, j, k)
+    place_ref[...] = anchor * cap + jnp.sum(same.astype(ints), axis=1, keepdims=True, dtype=ints)
+
+    for k in range(3, 6):
+        arrive(0, k)
     for l in range(2):
         for r in range(part):
             blank(l, r)
@@ -306,41 +304,47 @@
         targets(a, col + 1 - 2 * core)
         for d in range(1, half):
             targets(a, behind(d))
-    for k in range(3, 6):
-        arrive(k)
+    @pl.when(based)
+    def _():
+        for k in range(6):
+            spread(core, row, k)
+            own(k).wait_recv()
+            spread(1 - core, row, k)
+
     for k in range(6):
-        own(k).wait_recv()
-        spread(1 - core, j, k)
-        for d in range(1, part):
-            spread(core, source(d), k)
+        collect(0, k)
+    for step in range(1, nrow - 1):
+        for k in range(6):
+            arrive(step, k)
+            collect(step, k)
     for a in range(2):
         for d in range(1, half):
             passed(a, d).wait_recv()
             targets(a, behind(d) + 1 - 2 * core)
+    for step in range(nrow - 1):
+        for k in range(6):
+            received(step, k)
     for k in range(6):
-        for d in range(1, part):
-            onward(d, k).wait_recv()
-            spread(1 - core, source(d), k)
-    for k in range(6):
-        own(k).wait_send()
-        for d in range(1, part):
-            along(d, k).wait_send()
-            onward(d, k).wait_send()
-    for a in range(2):
-        @pl.when(gives)
+        @pl.when(based)
         def _():
-            for k in range(3):
-                give(a, k).wait_send()
-
+            own(k).wait_send()
+
+        for step in range(nrow - 1):
+            for way in (1, -1):
+                @pl.when(sends(way, step))
+                def _():
+                    relay(way, step, k).wait_send()
+
+                @pl.when(wanted(way, step))
+                def _():
+                    onward(way, step, k).wait_send()
+    for a in range(2):
         beside(a).wait_send()
         list_on(a).wait_send()
         for d in range(1, half):
             opposite(a, d).wait_send()
             passed(a, d).wait_send()
-    for e in range(2):
-        @pl.when(e * part + row // 2 != row)
-        def _():
-            list_to(e).wait_send()
+    list_to(i).wait_send()
 
 
 def pair_kernel(tl_ref, sl_ref, lc_ref, near_ref, far_ref, v_ref, acc_ref, both_a, both_b, g_a, g_b):
@@ -460,8 +464,7 @@
         return pltpu.make_async_remote_copy(
             src_ref=src, dst_ref=dst, send_sem=send, recv_sem=recv, device_id=where, device_id_type=MESH)
 
-    rows = nrow // 2
-    keep_a = row // rows
+    keep_a = lax.rem(row, 2)
     order = (1 - keep_a, keep_a)
 
     def within(n, d, k):
@@ -479,7 +482,7 @@
             part.at[n, d - 1, k], got.at[n, at, k], vsend.at[n, at, k], vrecv.at[n, at, k], {"col": facing(d)})
 
     def exchange(k):
-        return remote(swap.at[0, k], swap.at[1, k], zsend.at[k], zrecv.at[k], {"row": lax.rem(row + rows, nrow)})
+        return remote(swap.at[0, k], swap.at[1, k], zsend.at[k], zrecv.at[k], {"row": row + 1 - 2 * keep_a})
 
     def total(n, k):
         within(n, 0, k).wait_recv()
@@ -560,8 +563,8 @@
             pltpu.VMEM((3, local, nodes), f32), pltpu.VMEM((local, nodes), f32), *[pltpu.VMEM(drop_clusters.shape[::-1], ints)] * 2,
             pltpu.VMEM((1, drop_owner.shape[0]), ints), *[pltpu.VMEM((1, slots), ints)] * 2, dma((8,)),
             pltpu.VMEM((8, slots), ints), pltpu.VMEM((2, 2, 8, slots), ints),
-            pltpu.VMEM((2, ncol, 3, local, nodes), f32), pltpu.VMEM((2, part, 6, local, nodes), f32),
-            *[dma((part - 1, 6))] * 4, *[dma((6,))] * 2, *[dma((2, 3))] * 2, *[dma((2,))] * 2,
+            pltpu.VMEM((2, ncol, 3, local, nodes), f32), pltpu.VMEM((2, nrow, 6, local, nodes), f32),
+            *[dma((2 * nrow - 2, 6))] * 4, *[dma((6,))] * 2, *[dma((2,))] * 2,
             *[dma((max(half - 1, 1), 2))] * 4, *[dma((2,))] * 4],
         compiler_params=pltpu.CompilerParams(collective_id=0, has_side_effects=True, vmem_limit_bytes=30 << 20),
         name="gather_blocks",

time: 69.4 us -> 65.4 us (0.942)
  Pallas kernels: 68.2 us -> 64.5 us
    pallas_call x1, Pallas kernels: 36.4 us -> 29.5 us  [per_device(): pl.pallas_call(functools.partial(home_kernel, nrow, ncol, cap), out_shape...]
    pallas_call x1, Pallas kernels: 13.2 us -> 14.8 us  [per_device(): pl.pallas_call(pair_kernel, out_shape=pltpu.VMEM((2, ncol, 3, local, node...]
    pallas_call x1, Pallas kernels: 18.6 us -> 20.2 us  [per_device(): pl.pallas_call(functools.partial(gather_kernel, nrow, ncol, cap), out_sha...]
where the time goes in v5:
time: 65.4 us; the launch traced here: 65.9 us
  Pallas kernels  64.5 us (99%)
  local copies, waits for them, and re-layouts  0.68 us (1%)
  between operations  0.67 us (1%)
    pallas_call x1, Pallas kernels, per_device(): pl.pallas_call(functools.partial(home_kernel, nrow, ncol, cap), out_shape...  29.5 us
    pallas_call x1, Pallas kernels, per_device(): pl.pallas_call(functools.partial(gather_kernel, nrow, ncol, cap), out_sha...  20.2 us
    pallas_call x1, Pallas kernels, per_device(): pl.pallas_call(pair_kernel, out_shape=pltpu.VMEM((2, ncol, 3, local, node...  14.8 us

profile of v5, /device:TPU:0, one launch (start us, length us, event | category | flops | bytes accessed | tf_op | source)
XLA Modules:
  0.0 65.9 jit_solution(17633185094751419879)
XLA Ops:
  0.7 20.2 %gather_blocks.1 = (f32[8192,128]{1,0:T(8,128)S(1)}, f32[4096,128]{1,0:T(8,128)S(1)}, s32[4,512]{1,0:T(4,128)S(1)}, s32[4,512]{1,0:T(4,128)S(1)}, s32[4,128]{1,0...) custom-call(f32[3,128,128]{2,1,0:T(8,128)} %bitcast.7, f32[3,128,128]{2,1,0:T(8,128)} %bitcast.8, ...), custom_call_target="tpu_custom_call" | custom-call | tf_op jit(solution)/shard_map/gather_blocks/pallas_call | solution.py:555
  20.9 14.8 %pairs.1.v_ref = f32[2,4,3,128,128]{4,3,2,1,0:T(8,128)S(1)} custom-call(s32[4,512]{1,0:T(4,128)S(1)} %get-tuple-element.16.tl_ref, s32[4,512]{1,0:T(4,128)S(1)} %get-tuple-element.17.sl_ref, s32[4,128]{1,0:T(4,128)S(1)} %get-tuple-element.18.lc_ref, f32[8192,128]{1,0:T(8,128)S(1)} %get-tuple-element.19.near_ref, f32[4096,128]{1,0:T(8,128)S(1)} %get-tuple-element.20.far_ref), custom_call_target="tpu_custom_call" | custom-call | tf_op jit(solution)/shard_map/pairs/pallas_call | solution.py:573
  35.7 29.5 %to_owners.1 = f32[3,128,128]{2,1,0:T(8,128)S(1)} custom-call(s32[1,128]{1,0:T(1,128)S(1)} %get-tuple-element.13.slot_ref, s32[128,1]{1,0:T(8,128)S(1)} %get-tuple-element.14.place_ref, s32[128,1]{1,0:T(8,128)S(1)} %get-tuple-element.15.cnt_ref, f32[2,4,3,128,128]{4,3,2,1,0:T(8,128)S(1)} %pairs.1.v_ref), custom_call_target="tpu_custom_call" | custom-call | tf_op jit(solution)/shard_map/to_owners/pallas_call | solution.py:582
  65.2 0.7 %copy.12 = f32[128,3,128]{2,0,1:T(8,128)} copy(f32[128,3,128]{2,0,1:T(8,128)S(1)} %bitcast.6) | data formatting | bytes 393216

commit v6 on v5

--- a/solution.py
+++ b/solution.py
@@ -435,7 +435,20 @@
         speeds(2 * i, both_a, g_a)
         return carry
 
-    lax.fori_loop(0, (n + unroll - 1) // unroll // 2 + 1, many, 0)
+    blocks = (n + unroll - 1) // unroll
+    lax.fori_loop(0, blocks // 2, many, 0)
+    tail = lax.rem(blocks, 2) == 1
+
+    @pl.when(tail)
+    def _():
+        distances(blocks - 1, both_a, g_a)
+        speeds(blocks - 2, both_b, g_b)
+        speeds(blocks - 1, both_a, g_a)
+
+    @pl.when(jnp.logical_not(tail))
+    def _():
+        speeds(blocks - 1, both_b, g_b)
+
     for a in range(2):
         for c in range(ncol):
             for k in range(3):
@@ -502,8 +515,8 @@
 
     pick = (lax.broadcasted_iota(ints, (devs * cap, local), 0) == slot_ref[...]).astype(f32).astype(bf16)
     pl.semaphore_wait(barrier, devs - 1)
-    for n in range(2):
-        for k in range(3):
+    for k in range(3):
+        for n in range(2):
             for d in [*range(1, half), 0]:
                 within(n, d, k).start()
 
@@ -513,19 +526,23 @@
             part[n, d - 1, k] = v_ref[order[n], facing(d), k] + got[n, d, k]
             across(n, d, k).start()
 
-    for k in range(3):
-        pass_on(0, k)
-    for k in range(3):
-        swap[0, k] = total(0, k)
-        exchange(k).start()
-        pass_on(1, k)
-    for k in range(3):
+    def finish(k):
         mine = total(1, k)
         exchange(k).wait_recv()
         outg[k] = move(pick, mine + swap[1, k]).reshape(devs, cap, 128)
         for d in range(1, devs):
             deal(d, k).start()
         arr[k, me] = outg[k, me]
+
+    for k in range(3):
+        pass_on(0, k)
+        pass_on(1, k)
+    for k in range(3):
+        swap[0, k] = total(0, k)
+        exchange(k).start()
+        if k > 0:
+            finish(k - 1)
+    finish(2)
     fetch = (lax.broadcasted_iota(ints, (local, devs * cap), 1) == place_ref[...]).astype(f32).astype(bf16)
     live = lax.broadcasted_iota(ints, (local, 128), 1) < cnt_ref[...]
     for k in range(3):

time: 65.4 us -> 62.4 us (0.954); the launches traced: 65.9 us -> 61.7 us
  Pallas kernels: 64.5 us -> 60.3 us
    pallas_call x1, Pallas kernels: 14.8 us -> 10.5 us  [per_device(): pl.pallas_call(pair_kernel, out_shape=pltpu.VMEM((2, ncol, 3, local, node...]
where the time goes in v6:
time: 62.4 us; the launch traced here: 61.7 us
  Pallas kernels  60.3 us (97%)
  local copies, waits for them, and re-layouts  0.68 us (1%)
  between operations  0.67 us (1%)
    pallas_call x1, Pallas kernels, per_device(): pl.pallas_call(functools.partial(home_kernel, nrow, ncol, cap), out_shape...  29.6 us
    pallas_call x1, Pallas kernels, per_device(): pl.pallas_call(functools.partial(gather_kernel, nrow, ncol, cap), out_sha...  20.2 us
    pallas_call x1, Pallas kernels, per_device(): pl.pallas_call(pair_kernel, out_shape=pltpu.VMEM((2, ncol, 3, local, node...  10.5 us

profile of v6, /device:TPU:0, one launch (start us, length us, event | category | flops | bytes accessed | tf_op | source)
XLA Modules:
  0.0 61.7 jit_solution(10433775447295370780)
XLA Ops:
  0.7 20.2 %gather_blocks.1 = (f32[8192,128]{1,0:T(8,128)S(1)}, f32[4096,128]{1,0:T(8,128)S(1)}, s32[4,512]{1,0:T(4,128)S(1)}, s32[4,512]{1,0:T(4,128)S(1)}, s32[4,128]{1,0...) custom-call(f32[3,128,128]{2,1,0:T(8,128)} %bitcast.7, f32[3,128,128]{2,1,0:T(8,128)} %bitcast.8, ...), custom_call_target="tpu_custom_call" | custom-call | tf_op jit(solution)/shard_map/gather_blocks/pallas_call | solution.py:572
  20.9 10.5 %pairs.1.v_ref = f32[2,4,3,128,128]{4,3,2,1,0:T(8,128)S(1)} custom-call(s32[4,512]{1,0:T(4,128)S(1)} %get-tuple-element.16.tl_ref, s32[4,512]{1,0:T(4,128)S(1)} %get-tuple-element.17.sl_ref, s32[4,128]{1,0:T(4,128)S(1)} %get-tuple-element.18.lc_ref, f32[8192,128]{1,0:T(8,128)S(1)} %get-tuple-element.19.near_ref, f32[4096,128]{1,0:T(8,128)S(1)} %get-tuple-element.20.far_ref), custom_call_target="tpu_custom_call" | custom-call | tf_op jit(solution)/shard_map/pairs/pallas_call | solution.py:590
  31.4 29.6 %to_owners.1 = f32[3,128,128]{2,1,0:T(8,128)S(1)} custom-call(s32[1,128]{1,0:T(1,128)S(1)} %get-tuple-element.13.slot_ref, s32[128,1]{1,0:T(8,128)S(1)} %get-tuple-element.14.place_ref, s32[128,1]{1,0:T(8,128)S(1)} %get-tuple-element.15.cnt_ref, f32[2,4,3,128,128]{4,3,2,1,0:T(8,128)S(1)} %pairs.1.v_ref), custom_call_target="tpu_custom_call" | custom-call | tf_op jit(solution)/shard_map/to_owners/pallas_call | solution.py:599
  61.0 0.7 %copy.12 = f32[128,3,128]{2,0,1:T(8,128)} copy(f32[128,3,128]{2,0,1:T(8,128)S(1)} %bitcast.6) | data formatting | bytes 393216

commit v7 on v6

--- a/solution.py
+++ b/solution.py
@@ -379,8 +379,8 @@
     def tile(i):
         return pl.ds(pl.multiple_of(i * 8, 8), 8)
 
-    def distances(block, both_ref, g_ref):
-        for u in range(unroll):
+    def distances(block, both_ref, g_ref, us=range(unroll)):
+        for u in us:
             j = block * unroll + u
             l, e = entry(j)
             t, s = tl_ref[l, e], sl_ref[l, e]
@@ -409,8 +409,8 @@
             both_ref[u] = lax.dot_general(left, weights, (((0,), (0,)), ((), ())), preferred_element_type=f32)
             g_ref[u] = jnp.concatenate([jnp.where(last, 1.0, hi), jnp.where(last, 0.0, mid)], axis=0).astype(bf16)
 
-    def speeds(block, both_ref, g_ref):
-        for u in range(unroll):
+    def speeds(block, both_ref, g_ref, us=range(unroll)):
+        for u in us:
             l, e = entry(block * unroll + u)
             t = tl_ref[l, e]
             both, g = both_ref[u], g_ref[u]
@@ -429,10 +429,12 @@
             acc_ref[tile(t), :] += pltpu.roll(from_iso, 4, 0) + near_ref[tile(t), :] * from_pro[3:4] + 0.5 * from_pro
 
     def many(i, carry):
-        distances(2 * i, both_a, g_a)
-        speeds(2 * i - 1, both_b, g_b)
-        distances(2 * i + 1, both_b, g_b)
-        speeds(2 * i, both_a, g_a)
+        for u in range(unroll):
+            distances(2 * i, both_a, g_a, [u])
+            speeds(2 * i - 1, both_b, g_b, [u])
+        for u in range(unroll):
+            distances(2 * i + 1, both_b, g_b, [u])
+            speeds(2 * i, both_a, g_a, [u])
         return carry
 
     blocks = (n + unroll - 1) // unroll

time: 62.4 us -> 61.5 us (0.986)
    pallas_call x1, Pallas kernels: 29.6 us -> 27.2 us  [per_device(): pl.pallas_call(functools.partial(home_kernel, nrow, ncol, cap), out_shape...]
    pallas_call x1, Pallas kernels: 10.5 us -> 12.4 us  [per_device(): pl.pallas_call(pair_kernel, out_shape=pltpu.VMEM((2, ncol, 3, local, node...]
where the time goes in v7:
time: 61.5 us; the launch traced here: 61.1 us
  Pallas kernels  59.8 us (97%)
  local copies, waits for them, and re-layouts  0.68 us (1%)
  between operations  0.67 us (1%)
    pallas_call x1, Pallas kernels, per_device(): pl.pallas_call(functools.partial(home_kernel, nrow, ncol, cap), out_shape...  27.2 us
    pallas_call x1, Pallas kernels, per_device(): pl.pallas_call(functools.partial(gather_kernel, nrow, ncol, cap), out_sha...  20.2 us
    pallas_call x1, Pallas kernels, per_device(): pl.pallas_call(pair_kernel, out_shape=pltpu.VMEM((2, ncol, 3, local, node...  12.4 us

profile of v7, /device:TPU:0, one launch (start us, length us, event | category | flops | bytes accessed | tf_op | source)
XLA Modules:
  0.0 61.1 jit_solution(4676034728847291116)
XLA Ops:
  0.7 20.2 %gather_blocks.1 = (f32[8192,128]{1,0:T(8,128)S(1)}, f32[4096,128]{1,0:T(8,128)S(1)}, s32[4,512]{1,0:T(4,128)S(1)}, s32[4,512]{1,0:T(4,128)S(1)}, s32[4,128]{1,0...) custom-call(f32[3,128,128]{2,1,0:T(8,128)} %bitcast.7, f32[3,128,128]{2,1,0:T(8,128)} %bitcast.8, ...), custom_call_target="tpu_custom_call" | custom-call | tf_op jit(solution)/shard_map/gather_blocks/pallas_call | solution.py:574
  20.9 12.4 %pairs.1.v_ref = f32[2,4,3,128,128]{4,3,2,1,0:T(8,128)S(1)} custom-call(s32[4,512]{1,0:T(4,128)S(1)} %get-tuple-element.16.tl_ref, s32[4,512]{1,0:T(4,128)S(1)} %get-tuple-element.17.sl_ref, s32[4,128]{1,0:T(4,128)S(1)} %get-tuple-element.18.lc_ref, f32[8192,128]{1,0:T(8,128)S(1)} %get-tuple-element.19.near_ref, f32[4096,128]{1,0:T(8,128)S(1)} %get-tuple-element.20.far_ref), custom_call_target="tpu_custom_call" | custom-call | tf_op jit(solution)/shard_map/pairs/pallas_call | solution.py:592
  33.3 27.2 %to_owners.1 = f32[3,128,128]{2,1,0:T(8,128)S(1)} custom-call(s32[1,128]{1,0:T(1,128)S(1)} %get-tuple-element.13.slot_ref, s32[128,1]{1,0:T(8,128)S(1)} %get-tuple-element.14.place_ref, s32[128,1]{1,0:T(8,128)S(1)} %get-tuple-element.15.cnt_ref, f32[2,4,3,128,128]{4,3,2,1,0:T(8,128)S(1)} %pairs.1.v_ref), custom_call_target="tpu_custom_call" | custom-call | tf_op jit(solution)/shard_map/to_owners/pallas_call | solution.py:601
  60.5 0.7 %copy.12 = f32[128,3,128]{2,0,1:T(8,128)} copy(f32[128,3,128]{2,0,1:T(8,128)S(1)} %bitcast.6) | data formatting | bytes 393216

commit v8 on v7

--- a/solution.py
+++ b/solution.py
@@ -17,7 +17,7 @@
 
 
 HBM = pl.BlockSpec(memory_space=pltpu.HBM)
-unroll = 16
+unroll = 24
 f32, bf16, ints = jnp.float32, jnp.bfloat16, jnp.int32
 
 
@@ -313,15 +313,17 @@
 
     for k in range(6):
         collect(0, k)
+    for a in range(2):
+        for d in range(1, half):
+            passed(a, d).wait_recv()
+            targets(a, behind(d) + 1 - 2 * core)
+    for k in range(6):
+        received(0, k)
     for step in range(1, nrow - 1):
         for k in range(6):
             arrive(step, k)
             collect(step, k)
-    for a in range(2):
-        for d in range(1, half):
-            passed(a, d).wait_recv()
-            targets(a, behind(d) + 1 - 2 * core)
-    for step in range(nrow - 1):
+    for step in range(1, nrow - 1):
         for k in range(6):
             received(step, k)
     for k in range(6):
@@ -458,7 +460,7 @@
 
 
 def home_kernel(
-        nrow, ncol, cap, slot_ref, place_ref, cnt_ref, v_ref, out_ref, got, part, swap, outg, arr, vsend, vrecv, zsend, zrecv, asend, arecv):
+        nrow, ncol, cap, slot_ref, place_ref, cnt_ref, v_ref, out_ref, got, part, swap, ahead, outg, arr, vsend, vrecv, zsend, zrecv, esend, erecv, asend, arecv):
     row, col = lax.axis_index("row"), lax.axis_index("col")
     local = out_ref.shape[1]
     devs = nrow * ncol
@@ -499,6 +501,12 @@
     def exchange(k):
         return remote(swap.at[0, k], swap.at[1, k], zsend.at[k], zrecv.at[k], {"row": row + 1 - 2 * keep_a})
 
+    def early(d, k):
+        return remote(ahead.at[0, d], ahead.at[1, d], esend.at[d], erecv.at[d], {"row": row + 1 - 2 * keep_a})
+
+    def block_at(d):
+        return col if d == 0 else facing(d)
+
     def total(n, k):
         within(n, 0, k).wait_recv()
         mine = v_ref[order[n], col, k] + got[n, 0, k]
@@ -517,10 +525,9 @@
 
     pick = (lax.broadcasted_iota(ints, (devs * cap, local), 0) == slot_ref[...]).astype(f32).astype(bf16)
     pl.semaphore_wait(barrier, devs - 1)
-    for k in range(3):
-        for n in range(2):
-            for d in [*range(1, half), 0]:
-                within(n, d, k).start()
+    for n, k in [(0, 2), (0, 0), (1, 0), (0, 1), (1, 1), (1, 2)]:
+        for d in [*range(1, half), 0]:
+            within(n, d, k).start()
 
     def pass_on(n, k):
         for d in range(1, half):
@@ -528,36 +535,64 @@
             part[n, d - 1, k] = v_ref[order[n], facing(d), k] + got[n, d, k]
             across(n, d, k).start()
 
+    def rows_first(k):
+        for d in [*range(1, half), 0]:
+            within(0, d, k).wait_recv()
+            ahead[0, d] = v_ref[order[0], block_at(d), k] + got[0, d, k]
+            early(d, k).start()
+
+    def then_columns(k):
+        for d in range(1, half):
+            within(1, d, k).wait_recv()
+            early(d, k).wait_recv()
+            part[1, d - 1, k] = v_ref[order[1], facing(d), k] + got[1, d, k] + ahead[1, d]
+            across(1, d, k).start()
+
+    def spread_out(k, mine):
+        outg[k] = move(pick, mine).reshape(devs, cap, 128)
+        for d in range(1, devs):
+            deal(d, k).start()
+        arr[k, me] = outg[k, me]
+
+    def columns_first(k):
+        swap[0, k] = total(0, k)
+        exchange(k).start()
+
     def finish(k):
         mine = total(1, k)
         exchange(k).wait_recv()
-        outg[k] = move(pick, mine + swap[1, k]).reshape(devs, cap, 128)
-        for d in range(1, devs):
-            deal(d, k).start()
-        arr[k, me] = outg[k, me]
-
-    for k in range(3):
-        pass_on(0, k)
-        pass_on(1, k)
-    for k in range(3):
-        swap[0, k] = total(0, k)
-        exchange(k).start()
-        if k > 0:
-            finish(k - 1)
-    finish(2)
+        spread_out(k, mine + swap[1, k])
+
+    rows_first(2)
+    pass_on(0, 0)
+    pass_on(1, 0)
+    pass_on(0, 1)
+    pass_on(1, 1)
+    columns_first(0)
+    then_columns(2)
+    finish(0)
+    columns_first(1)
+    finish(1)
+    mine = total(1, 2)
+    early(0, 2).wait_recv()
+    spread_out(2, mine + ahead[1, 0])
     fetch = (lax.broadcasted_iota(ints, (local, devs * cap), 1) == place_ref[...]).astype(f32).astype(bf16)
     live = lax.broadcasted_iota(ints, (local, 128), 1) < cnt_ref[...]
     for k in range(3):
         for d in range(1, devs):
             deal(d, k).wait_recv()
         out_ref[k] = jnp.where(live, move(fetch, arr[k].reshape(devs * cap, 128)), 0.0)
+    for d in range(half):
+        early(d, 2).wait_send()
     for k in range(3):
-        exchange(k).wait_send()
+        if k != 2:
+            exchange(k).wait_send()
         for n in range(2):
             for d in range(half):
                 within(n, d, k).wait_send()
-            for d in range(1, half):
-                across(n, d, k).wait_send()
+            if k != 2 or n == 1:
+                for d in range(1, half):
+                    across(n, d, k).wait_send()
         for d in range(1, devs):
             deal(d, k).wait_send()
 
@@ -604,9 +639,9 @@
         in_specs=[VMEM] * 4, out_specs=VMEM,
         scratch_shapes=[
             pltpu.VMEM((2, ncol - 1, 3, local, nodes), f32), pltpu.VMEM((2, max(half - 1, 1), 3, local, nodes), f32),
-            pltpu.VMEM((2, 3, local, nodes), f32),
+            pltpu.VMEM((2, 3, local, nodes), f32), pltpu.VMEM((2, half, local, nodes), f32),
             pltpu.VMEM((3, devs, cap, nodes), f32), pltpu.VMEM((3, devs, cap, nodes), f32),
-            dma((2, ncol - 1, 3)), dma((2, ncol - 1, 3)), dma((3,)), dma((3,)), dma((devs - 1, 3)), dma((devs - 1, 3)),
+            dma((2, ncol - 1, 3)), dma((2, ncol - 1, 3)), dma((3,)), dma((3,)), dma((half,)), dma((half,)), dma((devs - 1, 3)), dma((devs - 1, 3)),
         ],
         compiler_params=pltpu.CompilerParams(collective_id=1, has_side_effects=True, vmem_limit_bytes=30 << 20),
         name="to_owners",

time: 61.5 us -> 61.7 us (level)
    pallas_call x1, Pallas kernels: 12.4 us -> 13.2 us  [per_device(): pl.pallas_call(pair_kernel, out_shape=pltpu.VMEM((2, ncol, 3, local, node...]
where the time goes in v8:
time: 61.7 us; the launch traced here: 61.6 us
  Pallas kernels  60.3 us (98%)
  local copies, waits for them, and re-layouts  0.68 us (1%)
  between operations  0.67 us (1%)
    pallas_call x1, Pallas kernels, per_device(): pl.pallas_call(functools.partial(home_kernel, nrow, ncol, cap), out_shape...  26.8 us
    pallas_call x1, Pallas kernels, per_device(): pl.pallas_call(functools.partial(gather_kernel, nrow, ncol, cap), out_sha...  20.2 us
    pallas_call x1, Pallas kernels, per_device(): pl.pallas_call(pair_kernel, out_shape=pltpu.VMEM((2, ncol, 3, local, node...  13.2 us

profile of v8, /device:TPU:0, one launch (start us, length us, event | category | flops | bytes accessed | tf_op | source)
XLA Modules:
  0.0 61.6 jit_solution(10259860948822432418)
XLA Ops:
  0.7 20.2 %gather_blocks.1 = (f32[8192,128]{1,0:T(8,128)S(1)}, f32[4096,128]{1,0:T(8,128)S(1)}, s32[4,512]{1,0:T(4,128)S(1)}, s32[4,512]{1,0:T(4,128)S(1)}, s32[4,128]{1,0...) custom-call(f32[3,128,128]{2,1,0:T(8,128)} %bitcast.7, f32[3,128,128]{2,1,0:T(8,128)} %bitcast.8, ...), custom_call_target="tpu_custom_call" | custom-call | tf_op jit(solution)/shard_map/gather_blocks/pallas_call | solution.py:609
  20.9 13.2 %pairs.1.v_ref = f32[2,4,3,128,128]{4,3,2,1,0:T(8,128)S(1)} custom-call(s32[4,512]{1,0:T(4,128)S(1)} %get-tuple-element.16.tl_ref, s32[4,512]{1,0:T(4,128)S(1)} %get-tuple-element.17.sl_ref, s32[4,128]{1,0:T(4,128)S(1)} %get-tuple-element.18.lc_ref, f32[8192,128]{1,0:T(8,128)S(1)} %get-tuple-element.19.near_ref, f32[4096,128]{1,0:T(8,128)S(1)} %get-tuple-element.20.far_ref), custom_call_target="tpu_custom_call" | custom-call | tf_op jit(solution)/shard_map/pairs/pallas_call | solution.py:627
  34.1 26.8 %to_owners.1 = f32[3,128,128]{2,1,0:T(8,128)S(1)} custom-call(s32[1,128]{1,0:T(1,128)S(1)} %get-tuple-element.13.slot_ref, s32[128,1]{1,0:T(8,128)S(1)} %get-tuple-element.14.place_ref, s32[128,1]{1,0:T(8,128)S(1)} %get-tuple-element.15.cnt_ref, f32[2,4,3,128,128]{4,3,2,1,0:T(8,128)S(1)} %pairs.1.v_ref), custom_call_target="tpu_custom_call" | custom-call | tf_op jit(solution)/shard_map/to_owners/pallas_call | solution.py:636
  61.0 0.7 %copy.12 = f32[128,3,128]{2,0,1:T(8,128)} copy(f32[128,3,128]{2,0,1:T(8,128)S(1)} %bitcast.6) | data formatting | bytes 393216

commit v9 on v8

--- a/solution.py
+++ b/solution.py
@@ -17,7 +17,7 @@
 
 
 HBM = pl.BlockSpec(memory_space=pltpu.HBM)
-unroll = 24
+unroll = 16
 f32, bf16, ints = jnp.float32, jnp.bfloat16, jnp.int32
 
 
@@ -62,13 +62,13 @@
     loads = [pltpu.make_async_copy(src, dst, here_sem.at[n]) for n, (src, dst) in enumerate((
         (pos_in, pos_ref), (tgt_in, tgt_ref), (src_in, src_ref), (dct_in, dct_ref), (nct_in, nct_ref), (own_in, own_ref),
         (curv_in, curv_ref), (nrm_in, nrm_ref)))]
-    for load in loads:
-        load.start()
     barrier = pltpu.get_barrier_semaphore()
     for d in range(1, nrow):
         pl.semaphore_signal(barrier, inc=1, device_id={"row": lax.rem(row + d, nrow)}, device_id_type=MESH)
     for d in range(1, ncol):
         pl.semaphore_signal(barrier, inc=1, device_id={"col": lax.rem(col + d, ncol)}, device_id_type=MESH)
+    for load in loads:
+        load.start()
 
     def remote(src, dst, send, recv, where):
         return pltpu.make_async_remote_copy(

time: 61.7 us -> 61.9 us (level); the launches traced: 61.6 us -> 62.9 us
  Pallas kernels: 60.3 us -> 61.5 us
    pallas_call x1, Pallas kernels: 26.8 us -> 30.3 us  [per_device(): pl.pallas_call(functools.partial(home_kernel, nrow, ncol, cap), out_shape...]
    pallas_call x1, Pallas kernels: 13.2 us -> 11 us  [per_device(): pl.pallas_call(pair_kernel, out_shape=pltpu.VMEM((2, ncol, 3, local, node...]
where the time goes in v9:
time: 61.9 us; the launch traced here: 62.9 us
  Pallas kernels  61.5 us (99%)
  local copies, waits for them, and re-layouts  0.68 us (1%)
  between operations  0.67 us (1%)
    pallas_call x1, Pallas kernels, per_device(): pl.pallas_call(functools.partial(home_kernel, nrow, ncol, cap), out_shape...  30.3 us
    pallas_call x1, Pallas kernels, per_device(): pl.pallas_call(functools.partial(gather_kernel, nrow, ncol, cap), out_sha...  20.2 us
    pallas_call x1, Pallas kernels, per_device(): pl.pallas_call(pair_kernel, out_shape=pltpu.VMEM((2, ncol, 3, local, node...  11 us

profile of v9, /device:TPU:0, one launch (start us, length us, event | category | flops | bytes accessed | tf_op | source)
XLA Modules:
  0.0 62.9 jit_solution(17150047954676985520)
XLA Ops:
  0.7 20.2 %gather_blocks.1 = (f32[8192,128]{1,0:T(8,128)S(1)}, f32[4096,128]{1,0:T(8,128)S(1)}, s32[4,512]{1,0:T(4,128)S(1)}, s32[4,512]{1,0:T(4,128)S(1)}, s32[4,128]{1,0...) custom-call(f32[3,128,128]{2,1,0:T(8,128)} %bitcast.7, f32[3,128,128]{2,1,0:T(8,128)} %bitcast.8, ...), custom_call_target="tpu_custom_call" | custom-call | tf_op jit(solution)/shard_map/gather_blocks/pallas_call | solution.py:609
  20.8 11.0 %pairs.1.v_ref = f32[2,4,3,128,128]{4,3,2,1,0:T(8,128)S(1)} custom-call(s32[4,512]{1,0:T(4,128)S(1)} %get-tuple-element.16.tl_ref, s32[4,512]{1,0:T(4,128)S(1)} %get-tuple-element.17.sl_ref, s32[4,128]{1,0:T(4,128)S(1)} %get-tuple-element.18.lc_ref, f32[8192,128]{1,0:T(8,128)S(1)} %get-tuple-element.19.near_ref, f32[4096,128]{1,0:T(8,128)S(1)} %get-tuple-element.20.far_ref), custom_call_target="tpu_custom_call" | custom-call | tf_op jit(solution)/shard_map/pairs/pallas_call | solution.py:627
  31.9 30.3 %to_owners.1 = f32[3,128,128]{2,1,0:T(8,128)S(1)} custom-call(s32[1,128]{1,0:T(1,128)S(1)} %get-tuple-element.13.slot_ref, s32[128,1]{1,0:T(8,128)S(1)} %get-tuple-element.14.place_ref, s32[128,1]{1,0:T(8,128)S(1)} %get-tuple-element.15.cnt_ref, f32[2,4,3,128,128]{4,3,2,1,0:T(8,128)S(1)} %pairs.1.v_ref), custom_call_target="tpu_custom_call" | custom-call | tf_op jit(solution)/shard_map/to_owners/pallas_call | solution.py:636
  62.2 0.7 %copy.12 = f32[128,3,128]{2,0,1:T(8,128)} copy(f32[128,3,128]{2,0,1:T(8,128)S(1)} %bitcast.6) | data formatting | bytes 393216
